TPU v7x, 32 devices: a whole 2x2x4 slice. The times are simulated.
32 devices in a mesh: col: 4 (over x, core), depth: 8 (over z, y).
Axes of the slice: x: 2, y: 2, z: 4, core: 2. Of those that a mesh axis runs over, the one named last changes fastest.
Arguments:
- density: float32 [64, 512, 1024], P('depth', 'col'), may hold values from -6 to 6
- offsets: int32 [64], P('depth'), may hold values from 0 to 8, as said below
- view_flip: int32 [512], P('col'), may hold values from 0 to 1
Outputs:
- image: float32 [4, 512, 1024], P(None, ('col', 'depth'))
Inputs may be any that keep to these rules, and one draw needn't show every extreme that they name: `offsets`: in every block of 8 consecutive slices (those of one device) one slice has offset 8 and another offset 0. `view_flip`: 0: slices of lower depth index lie in front for that column; 1: the reverse.
All inputs are finite; a program needn't handle non-finite values.
Results may differ from a plain program's by a relative error of at most 0.00036.
Values may be sent and summed in bfloat16 or wider, within the bound.
A program may use at most 128 MiB of HBM per device.

v0:
```python
import jax
import jax.numpy as jnp
from jax import lax
from jax.sharding import PartitionSpec as P

SMAX = 8


def extended_2(block, sides, width):
    for axis, dim in sides:
        count = lax.axis_size(axis)
        forward = [(i, i + 1) for i in range(count - 1)]
        backward = [(target, source) for source, target in forward]
        low = lax.ppermute(
            lax.slice_in_dim(block, block.shape[dim] - width, None, axis=dim), axis, forward
        )
        high = lax.ppermute(lax.slice_in_dim(block, 0, width, axis=dim), axis, backward)
        block = jnp.concatenate([low, block, high], axis=dim)
    return block


def from_behind(value, axis, steps):
    count = lax.axis_size(axis)
    leading, last = (max(0, -steps), min(count, count - steps))
    return lax.ppermute(value, axis, [(source, source + steps) for source in range(leading, last)])


def partner(block, axis, apart):
    count = lax.axis_size(axis)
    route = []
    for low in range(count):
        high = low | 1 << apart
        if high != low and high < count:
            route += [(low, high), (high, low)]
    return lax.ppermute(block, axis, route)


def shade_cells(extended, absorb):
    center = extended[1:-1, 1:-1]
    slope_z = (extended[2:, 1:-1] - extended[:-2, 1:-1]) * 0.5
    slope_x = (extended[1:-1, 2:] - extended[1:-1, :-2]) * 0.5
    padded_y = jnp.pad(center, ((0, 0), (0, 0), (1, 1)))
    slope_y = (padded_y[..., 2:] - padded_y[..., :-2]) * 0.5
    square = slope_x * slope_x + slope_y * slope_y + slope_z * slope_z
    lambert = (0.48 * slope_x + 0.6 * slope_y + 0.64 * slope_z) / jnp.sqrt(jnp.maximum(square, 1.0))
    lighting = 0.2 + 0.8 * jnp.abs(lambert)
    center_sq = center * center
    opacity = 1.0 - jnp.exp(-absorb * center_sq * center_sq)
    weight = opacity * lighting
    red_part = weight * jax.nn.sigmoid(2.0 * center)
    green_part = weight * jax.nn.sigmoid(1.0 - center_sq)
    blue_part = weight * jax.nn.sigmoid(-2.0 * center)
    return jnp.stack([red_part, green_part, blue_part, opacity], axis=1).astype(jnp.bfloat16)


def interp_matrix(order_size):
    row_ids = jnp.arange(order_size, dtype=jnp.int32)[:, None]
    col_ids = jnp.arange(order_size, dtype=jnp.int32)[None, :]
    distance = jnp.abs(row_ids - col_ids)
    values = jnp.where(
        distance == 0, 0.5, jnp.where(distance == 1, 0.1875, jnp.where(distance == 2, 0.0625, 0.0))
    )
    return values.astype(jnp.bfloat16)


def on_device(density, offsets, view_flip):
    depth_count = lax.axis_size("depth")
    slices, columns, height = density.shape
    absorb = 0.5 / (slices * depth_count)
    widest = SMAX
    with_depth = extended_2(density, (("depth", 0),), 1)
    with_rims = extended_2(with_depth, (("col", 1),), 1)
    shaded = shade_cells(with_rims, absorb)
    from_left = from_behind(shaded[:, :, columns - widest :], "col", 1)
    widened = jnp.concatenate([from_left, shaded], axis=2)
    interp = interp_matrix(height)
    anchor = jnp.zeros((), jnp.int32)

    def advance(carried, visit):
        colour_front, colour_back, transmit = carried
        plane = lax.dynamic_index_in_dim(widened, visit, 0, keepdims=False)
        start = widest - offsets[visit]
        sheared = lax.dynamic_slice(plane, (anchor, start, anchor), (4, columns, height))
        resampled = jnp.dot(
            sheared.reshape(4 * columns, height), interp, preferred_element_type=jnp.float32
        ).reshape(4, columns, height)
        colour_front = colour_front + transmit[None] * resampled[:3]
        colour_back = resampled[:3] + (1.0 - resampled[3])[None] * colour_back
        transmit = transmit * (1.0 - resampled[3])
        return ((colour_front, colour_back, transmit), None)

    blank = jnp.zeros((3, columns, height), jnp.float32)
    initial = (blank, blank, jnp.ones((columns, height), jnp.float32))
    (colour_front, colour_back, transmit), _ = lax.scan(
        advance, initial, jnp.arange(slices, dtype=jnp.int32)
    )
    colour = jnp.where(view_flip[None, :, None] == 0, colour_front, colour_back)
    opacity = 1.0 - transmit
    block_width = columns // depth_count
    flag_blocks = view_flip.reshape(depth_count, block_width)
    partial_value = jnp.concatenate([colour, opacity[None]], axis=0).reshape(
        4, depth_count, block_width, height
    )
    flags = flag_blocks
    position = lax.axis_index("depth")
    for section in range(depth_count.bit_length() - 1):
        halves = partial_value.reshape(4, partial_value.shape[1] // 2, 2, block_width, height)
        flag_halves = flags.reshape(flags.shape[0] // 2, 2, block_width)
        upper = position // 2**section % 2 == 1
        kept = jnp.where(upper, halves[:, :, 1], halves[:, :, 0])
        outgoing = jnp.where(upper, halves[:, :, 0], halves[:, :, 1])
        flags = jnp.where(upper, flag_halves[:, 1], flag_halves[:, 0])
        received = partner(outgoing, "depth", section)
        view_front = (flags == 0)[None, :, :, None]
        mine_first = jnp.logical_not(upper) == view_front
        in_front = jnp.where(mine_first, kept, received)
        behind = jnp.where(mine_first, received, kept)
        partial_value = in_front + (1.0 - in_front[3:4]) * behind
    return partial_value.reshape(4, block_width, height)


def solution(mesh):
    in_specs = (P("depth", "col", None), P("depth"), P("col"))
    out_specs = P(None, ("col", "depth"), None)
    return jax.shard_map(
        on_device, mesh=mesh, in_specs=in_specs, out_specs=out_specs, check_vma=False
    )
```

profile of v0, /device:TPU:10, one launch (start us, length us, event | category | flops | bytes accessed | tf_op | source)
XLA Modules:
  0.0 227.8 jit_solution(12326767413153054748)
XLA Ops:
  1.3 3.4 %collective-permute-start = (f32[1,128,1024]{2,1,0:T(8,128)S(1)}, f32[1,128,1024]{2,1,0:T(8,128)S(1)}, u32[]{:S(2)}, u32[]{:S(2)}) collective-permute-start(f32[1,128,1024]{2,1,0:T(8,128)S(1)} %get-tuple-element.193), channel_id=1, source_target_pairs={{0,1},{1,2},{2,3},{3,4},{4,5},{5,6},{6,7},{8,9},{9,10},{10,11},{11... | collective-permute-start | bytes 1572872 | tf_op jit(solution)/shard_map/ppermute | solution.py:14
  4.7 3.3 %collective-permute-start.1 = (f32[1,128,1024]{2,1,0:T(8,128)S(1)}, f32[1,128,1024]{2,1,0:T(8,128)S(1)}, u32[]{:S(2)}, u32[]{:S(2)}) collective-permute-start(f32[1,128,1024]{2,1,0:T(8,128)S(1)} %get-tuple-element.192), channel_id=1, source_target_pairs={{1,0},{2,1},{3,2},{4,3},{5,4},{6,5},{7,6},{9,8},{10,9},{11,10},{12... | collective-permute-start | bytes 1572872 | tf_op jit(solution)/shard_map/ppermute | solution.py:17
  8.0 19.1 %collective-permute-done = f32[1,128,1024]{2,1,0:T(8,128)S(1)} collective-permute-done((f32[1,128,1024]{2,1,0:T(8,128)S(1)}, f32[1,128,1024]{2,1,0:T(8,128)S(1)}, u32[]{:S(2)}, u32[]{:S(2)}) %collective-permute-start) | collective-permute-done | bytes 524320 | tf_op jit(solution)/shard_map/ppermute | solution.py:14
  27.2 2.7 %constant_dynamic-update-slice_fusion.1 = f32[10,128,1024]{2,1,0:T(8,128)S(1)} fusion(f32[10,128,1024]{2,1,0:T(8,128)S(1)} %constant_dynamic-update-slice_fusion.2, f32[8,128,1024]{2,1,0:T(8,128)} %param.5), kind=kLoop, calls=%fused_computation.81 | loop fusion | bytes 8388608
  30.0 1.9 collective-permute-start.2
  31.9 2.4 %collective-permute-start.3 = (f32[10,1,1024]{2,1,0:T(1,128)S(1)}, f32[10,1,1024]{2,1,0:T(1,128)S(1)}, u32[]{:S(2)}, u32[]{:S(2)}) collective-permute-start(f32[10,1,1024]{2,1,0:T(1,128)S(1)} %get-tuple-element.190), channel_id=1, source_target_pairs={{0,8},{8,16},{16,24},{1,9},{9,17},{17,25},{2,10},{10,18},{18,26},{... | collective-permute-start | bytes 122888 | tf_op jit(solution)/shard_map/ppermute | solution.py:14
  34.3 2.9 %collective-permute-done.3 = f32[10,1,1024]{2,1,0:T(1,128)S(1)} collective-permute-done((f32[10,1,1024]{2,1,0:T(1,128)S(1)}, f32[10,1,1024]{2,1,0:T(1,128)S(1)}, u32[]{:S(2)}, u32[]{:S(2)}) %collective-permute-start.3) | collective-permute-done | bytes 40992 | tf_op jit(solution)/shard_map/ppermute | solution.py:14
  37.2 9.7 %fusion.29 = (bf16[8,1,128,1024]{3,2,1,0:T(8,128)(2,1)S(1)}, f32[8,128,1024]{2,1,0:T(8,128)S(1)}) fusion(f32[8,128,1024]{2,1,0:T(8,128)S(1)} %copy-done, f32[1,128,1024]{2,1,0:T(8,128)S(1)} %collective-permute-done, f32[1,128,1024]{2,1,0:T(8,128)S(1)} %collective-permute-done.1, f32[10,128,1024]{2,1,0:T(8,128)S(1)} %constant_dynamic-update-slice_fusion, ...), kind=kLoop, calls=%fused_computation.49 | loop fusion | flops 37748736 | bytes 16859136 | tf_op jit(solution)/shard_map/stack | solution.py:53
  46.9 3.0 %fusion.31 = (bf16[8,1,128,1024]{3,2,1,0:T(8,128)(2,1)S(1)}, bf16[8,1,128,1024]{3,2,1,0:T(8,128)(2,1)S(1)}, bf16[8,1,128,1024]{3,2,1,0:T(8,128)(2,1)S(1)}) fusion(f32[8,128,1024]{2,1,0:T(8,128)S(1)} %get-tuple-element.183, f32[8,128,1024]{2,1,0:T(8,128)S(1)} %copy-done), kind=kLoop, calls=%fused_computation.51 | loop fusion | flops 17825792 | bytes 14680064 | tf_op jit(solution)/shard_map/stack | solution.py:53
  52.8 1.9 collective-permute-start.4
  54.8 8.8 %collective-permute-done.4 = bf16[8,4,8,1024]{3,2,1,0:T(8,128)(2,1)} collective-permute-done((bf16[8,4,8,1024]{3,2,1,0:T(8,128)(2,1)}, bf16[8,4,8,1024]{3,2,1,0:T(8,128)(2,1)}, u32[]{:S(2)}, u32[]{:S(2)}) %collective-permute-start.4) | collective-permute-done | bytes 524320 | tf_op jit(solution)/shard_map/ppermute | solution.py:25
  63.6 7.4 %maximum_maximum_fusion = bf16[8,4,136,1024]{3,2,1,0:T(8,128)(2,1)} fusion(bf16[8,1,128,1024]{3,2,1,0:T(8,128)(2,1)} %copy-done.6, bf16[8,1,128,1024]{3,2,1,0:T(8,128)(2,1)} %copy-done.5, bf16[8,1,128,1024]{3,2,1,0:T(8,128)(2,1)} %copy-done.4, bf16[8,1,128,1024]{3,2,1,0:T(8,128)(2,1)} %copy-done.3, bf16[8,4,8,1024]{3,2,1,0:T(8,128)(2,1)} %collective-permute-done.4), kind=kLoop, calls=%fused_computation.28 | loop fusion | flops 44564480 | bytes 17825792 | tf_op jit(solution)/shard_map/concatenate | solution.py:75
  70.9 108.6 %while.18 = (s32[]{:T(128)}, f32[3,128,1024]{2,1,0:T(8,128)S(1)}, f32[3,128,1024]{2,1,0:T(8,128)S(1)}, f32[128,1024]{1,0:T(8,128)}, s32[8]{0:T(128)S(1)}, /*inde...) while((s32[]{:T(128)}, f32[3,128,1024]{2,1,0:T(8,128)S(1)}, ...), condition=%wide.region_1.2_spmd.clone, body=%wide.region_0.1_spmd.clone.sunk | while | flops 1085931520 | bytes 19923224 | solution.py:94
  75.6 1.5 constant_dynamic-slice_fusion.2
  77.1 2.6 %fusion.47 = f32[512,1024]{1,0:T(8,128)} fusion(bf16[512,1024]{1,0:T(8,128)(2,1)S(1)} %bitcast.134), kind=kOutput, calls=%fused_computation.6.clone.1 | convolution fusion | flops 1083179008 | bytes 3145728 | tf_op jit(solution)/shard_map/while/body/eval_jaxpr/dot_general | solution.py:84
  79.7 2.1 fusion.48
  81.8 1.6 slice.237
  89.1 1.5 constant_dynamic-slice_fusion.2
  90.6 2.6 %fusion.47 = f32[512,1024]{1,0:T(8,128)} fusion(bf16[512,1024]{1,0:T(8,128)(2,1)S(1)} %bitcast.134), kind=kOutput, calls=%fused_computation.6.clone.1 | convolution fusion | flops 1083179008 | bytes 3145728 | tf_op jit(solution)/shard_map/while/body/eval_jaxpr/dot_general | solution.py:84
  93.2 2.2 fusion.48
  95.4 1.6 slice.237
  102.7 1.5 constant_dynamic-slice_fusion.2
  104.2 2.6 %fusion.47 = f32[512,1024]{1,0:T(8,128)} fusion(bf16[512,1024]{1,0:T(8,128)(2,1)S(1)} %bitcast.134), kind=kOutput, calls=%fused_computation.6.clone.1 | convolution fusion | flops 1083179008 | bytes 3145728 | tf_op jit(solution)/shard_map/while/body/eval_jaxpr/dot_general | solution.py:84
  106.8 2.2 fusion.48
  109.0 1.6 slice.237
  117.8 2.6 %fusion.47 = f32[512,1024]{1,0:T(8,128)} fusion(bf16[512,1024]{1,0:T(8,128)(2,1)S(1)} %bitcast.134), kind=kOutput, calls=%fused_computation.6.clone.1 | convolution fusion | flops 1083179008 | bytes 3145728 | tf_op jit(solution)/shard_map/while/body/eval_jaxpr/dot_general | solution.py:84
  120.4 2.2 fusion.48
  122.6 1.6 slice.237
  129.9 1.5 constant_dynamic-slice_fusion.2
  131.4 2.6 %fusion.47 = f32[512,1024]{1,0:T(8,128)} fusion(bf16[512,1024]{1,0:T(8,128)(2,1)S(1)} %bitcast.134), kind=kOutput, calls=%fused_computation.6.clone.1 | convolution fusion | flops 1083179008 | bytes 3145728 | tf_op jit(solution)/shard_map/while/body/eval_jaxpr/dot_general | solution.py:84
  134.0 2.2 fusion.48
  136.2 1.6 slice.237
  143.5 1.5 constant_dynamic-slice_fusion.2
  145.0 2.6 %fusion.47 = f32[512,1024]{1,0:T(8,128)} fusion(bf16[512,1024]{1,0:T(8,128)(2,1)S(1)} %bitcast.134), kind=kOutput, calls=%fused_computation.6.clone.1 | convolution fusion | flops 1083179008 | bytes 3145728 | tf_op jit(solution)/shard_map/while/body/eval_jaxpr/dot_general | solution.py:84
  147.6 2.2 fusion.48
  149.8 1.6 slice.237
  158.6 2.6 %fusion.47 = f32[512,1024]{1,0:T(8,128)} fusion(bf16[512,1024]{1,0:T(8,128)(2,1)S(1)} %bitcast.134), kind=kOutput, calls=%fused_computation.6.clone.1 | convolution fusion | flops 1083179008 | bytes 3145728 | tf_op jit(solution)/shard_map/while/body/eval_jaxpr/dot_general | solution.py:84
  161.2 2.2 fusion.48
  163.4 1.6 slice.237
  172.2 2.6 %fusion.47 = f32[512,1024]{1,0:T(8,128)} fusion(bf16[512,1024]{1,0:T(8,128)(2,1)S(1)} %bitcast.134), kind=kOutput, calls=%fused_computation.6.clone.1 | convolution fusion | flops 1083179008 | bytes 3145728 | tf_op jit(solution)/shard_map/while/body/eval_jaxpr/dot_general | solution.py:84
  174.8 2.2 fusion.48
  177.0 1.6 slice.237
  183.3 2.5 %collective-permute-start.5 = (f32[4,4,16,1024]{3,2,1,0:T(8,128)}, f32[4,4,16,1024]{3,2,1,0:T(8,128)S(1)}, u32[]{:S(2)}, u32[]{:S(2)}) collective-permute-start(f32[4,4,16,1024]{3,2,1,0:T(8,128)} %select_bitcast_fusion), channel_id=1, source_target_pairs={{0,1},{1,0},{2,3},{3,2},{4,5},{5,4},{6,7},{7,6},{8,9},{9,8},{10,11... | collective-permute-start | bytes 3145736 | tf_op jit(solution)/shard_map/ppermute | solution.py:35
  185.9 16.7 %collective-permute-done.5 = f32[4,4,16,1024]{3,2,1,0:T(8,128)S(1)} collective-permute-done((f32[4,4,16,1024]{3,2,1,0:T(8,128)}, f32[4,4,16,1024]{3,2,1,0:T(8,128)S(1)}, u32[]{:S(2)}, u32[]{:S(2)}) %collective-permute-start.5) | collective-permute-done | bytes 1048608 | tf_op jit(solution)/shard_map/ppermute | solution.py:35
  202.6 2.2 broadcast_select_fusion.2
  204.9 1.6 multiply_add_fusion
  207.1 11.5 %collective-permute-done.6 = f32[4,2,16,1024]{3,2,1,0:T(8,128)S(1)} collective-permute-done((f32[4,2,16,1024]{3,2,1,0:T(8,128)S(1)}, f32[4,2,16,1024]{3,2,1,0:T(8,128)S(1)}, u32[]{:S(2)}, u32[]{:S(2)}) %collective-permute-start.6) | collective-permute-done | bytes 524320 | tf_op jit(solution)/shard_map/ppermute | solution.py:35
  220.2 6.7 %collective-permute-done.7 = f32[4,1,16,1024]{3,2,0,1:T(8,128)S(1)} collective-permute-done((f32[4,1,16,1024]{3,2,0,1:T(8,128)S(1)}, f32[4,1,16,1024]{3,2,0,1:T(8,128)S(1)}, u32[]{:S(2)}, u32[]{:S(2)}) %collective-permute-start.7) | collective-permute-done | bytes 262176 | tf_op jit(solution)/shard_map/ppermute | solution.py:35
  (83 shorter events, 34.0 us)
Async XLA Ops:
  1.3 25.8 %collective-permute-start = (f32[1,128,1024]{2,1,0:T(8,128)S(1)}, f32[1,128,1024]{2,1,0:T(8,128)S(1)}, u32[]{:S(2)}, u32[]{:S(2)}) collective-permute-start(f32[1,128,1024]{2,1,0:T(8,128)S(1)} %get-tuple-element.193), channel_id=1, source_target_pairs={{0,1},{1,2},{2,3},{3,4},{4,5},{5,6},{6,7},{8,9},{9,10},{10,11},{11... | collective-permute-start | bytes 1572872 | tf_op jit(solution)/shard_map/ppermute | solution.py:14
  4.7 25.1 %collective-permute-start.1 = (f32[1,128,1024]{2,1,0:T(8,128)S(1)}, f32[1,128,1024]{2,1,0:T(8,128)S(1)}, u32[]{:S(2)}, u32[]{:S(2)}) collective-permute-start(f32[1,128,1024]{2,1,0:T(8,128)S(1)} %get-tuple-element.192), channel_id=1, source_target_pairs={{1,0},{2,1},{3,2},{4,3},{5,4},{6,5},{7,6},{9,8},{10,9},{11,10},{12... | collective-permute-start | bytes 1572872 | tf_op jit(solution)/shard_map/ppermute | solution.py:17
  27.2 10.1 %copy-start = (f32[8,128,1024]{2,1,0:T(8,128)S(1)}, f32[8,128,1024]{2,1,0:T(8,128)}, u32[]{:S(2)}) copy-start(f32[8,128,1024]{2,1,0:T(8,128)} %param.5) | copy-start | bytes 12582916
  30.0 4.3 %collective-permute-start.2 = (f32[10,1,1024]{2,1,0:T(1,128)S(1)}, f32[10,1,1024]{2,1,0:T(1,128)S(1)}, u32[]{:S(2)}, u32[]{:S(2)}) collective-permute-start(f32[10,1,1024]{2,1,0:T(1,128)S(1)} %get-tuple-element.189), channel_id=1, source_target_pairs={{8,0},{16,8},{24,16},{9,1},{17,9},{25,17},{10,2},{18,10},{26,18},{... | collective-permute-start | bytes 122888 | tf_op jit(solution)/shard_map/ppermute | solution.py:17
  31.9 5.3 %collective-permute-start.3 = (f32[10,1,1024]{2,1,0:T(1,128)S(1)}, f32[10,1,1024]{2,1,0:T(1,128)S(1)}, u32[]{:S(2)}, u32[]{:S(2)}) collective-permute-start(f32[10,1,1024]{2,1,0:T(1,128)S(1)} %get-tuple-element.190), channel_id=1, source_target_pairs={{0,8},{8,16},{16,24},{1,9},{9,17},{17,25},{2,10},{10,18},{18,26},{... | collective-permute-start | bytes 122888 | tf_op jit(solution)/shard_map/ppermute | solution.py:14
  46.9 3.1 %copy-start.3 = (bf16[8,1,128,1024]{3,2,1,0:T(8,128)(2,1)}, bf16[8,1,128,1024]{3,2,1,0:T(8,128)(2,1)S(1)}, u32[]{:S(2)}) copy-start(bf16[8,1,128,1024]{3,2,1,0:T(8,128)(2,1)S(1)} %get-tuple-element.182) | copy-start | bytes 6291460
  50.0 1.4 copy-start.4
  50.0 2.3 copy-start.5
  50.0 2.8 %copy-start.6 = (bf16[8,1,128,1024]{3,2,1,0:T(8,128)(2,1)}, bf16[8,1,128,1024]{3,2,1,0:T(8,128)(2,1)S(1)}, u32[]{:S(2)}) copy-start(bf16[8,1,128,1024]{3,2,1,0:T(8,128)(2,1)S(1)} %get-tuple-element.191) | copy-start | bytes 6291460
  50.0 4.7 %copy-start.10 = (s32[128]{0:T(128)S(1)}, s32[128]{0:T(128)}, u32[]{:S(2)}) copy-start(s32[128]{0:T(128)} %param.7) | copy-start | bytes 1540
  52.8 10.8 %collective-permute-start.4 = (bf16[8,4,8,1024]{3,2,1,0:T(8,128)(2,1)}, bf16[8,4,8,1024]{3,2,1,0:T(8,128)(2,1)}, u32[]{:S(2)}, u32[]{:S(2)}) collective-permute-start(bf16[8,4,8,1024]{3,2,1,0:T(8,128)(2,1)} %pad_maximum_fusion.5), channel_id=1, source_target_pairs={{0,8},{8,16},{16,24},{1,9},{9,17},{17,25},{2,10},{10,18},{18,26},{... | collective-permute-start | bytes 1572872 | tf_op jit(solution)/shard_map/ppermute | solution.py:25
  54.7 16.2 %copy-start.11 = (s32[8]{0:T(128)S(1)}, s32[8]{0:T(128)}, u32[]{:S(2)}) copy-start(s32[8]{0:T(128)} %param.6) | copy-start | bytes 100
  180.7 2.6 %copy-start.7 = (f32[128,1024]{1,0:T(8,128)}, f32[128,1024]{1,0:T(8,128)S(1)}, u32[]{:S(2)}) copy-start(f32[128,1024]{1,0:T(8,128)S(1)} %broadcast_subtract_fusion) | copy-start | bytes 1572868
  181.0 1.2 copy-start.1
  183.3 21.6 %copy-start.2 = (f32[3,128,1024]{2,1,0:T(8,128)S(1)}, f32[3,128,1024]{2,1,0:T(8,128)}, u32[]{:S(2)}) copy-start(f32[3,128,1024]{2,1,0:T(8,128)} %copy-done.1) | copy-start | bytes 4718596
  183.3 19.3 %collective-permute-start.5 = (f32[4,4,16,1024]{3,2,1,0:T(8,128)}, f32[4,4,16,1024]{3,2,1,0:T(8,128)S(1)}, u32[]{:S(2)}, u32[]{:S(2)}) collective-permute-start(f32[4,4,16,1024]{3,2,1,0:T(8,128)} %select_bitcast_fusion), channel_id=1, source_target_pairs={{0,1},{1,0},{2,3},{3,2},{4,5},{5,4},{6,7},{7,6},{8,9},{9,8},{10,11... | collective-permute-start | bytes 3145736 | tf_op jit(solution)/shard_map/ppermute | solution.py:35
  185.8 19.1 %copy-start.8 = (f32[128,1024]{1,0:T(8,128)S(1)}, f32[128,1024]{1,0:T(8,128)}, u32[]{:S(2)}) copy-start(f32[128,1024]{1,0:T(8,128)} %copy-done.7) | copy-start | bytes 1572868
  202.6 2.2 copy-start.9
  206.5 12.1 %collective-permute-start.6 = (f32[4,2,16,1024]{3,2,1,0:T(8,128)S(1)}, f32[4,2,16,1024]{3,2,1,0:T(8,128)S(1)}, u32[]{:S(2)}, u32[]{:S(2)}) collective-permute-start(f32[4,2,16,1024]{3,2,1,0:T(8,128)S(1)} %select_bitcast_fusion.1), channel_id=1, source_target_pairs={{0,2},{2,0},{1,3},{3,1},{4,6},{6,4},{5,7},{7,5},{8,10},{10,8},{9,1... | collective-permute-start | bytes 1572872 | tf_op jit(solution)/shard_map/ppermute | solution.py:35
  218.9 7.9 %collective-permute-start.7 = (f32[4,1,16,1024]{3,2,0,1:T(8,128)S(1)}, f32[4,1,16,1024]{3,2,0,1:T(8,128)S(1)}, u32[]{:S(2)}, u32[]{:S(2)}) collective-permute-start(f32[4,1,16,1024]{3,2,0,1:T(8,128)S(1)} %select_bitcast_fusion.2), channel_id=1, source_target_pairs={{0,4},{4,0},{1,5},{5,1},{2,6},{6,2},{3,7},{7,3},{8,12},{12,8},{9,1... | collective-permute-start | bytes 786440 | tf_op jit(solution)/shard_map/ppermute | solution.py:35
where the time goes:
time: 232 us; the launch traced here: 228 us
  waiting for transfers between devices  65.7 us (28%)
  other arithmetic  54.2 us (23%)
  local copies, waits for them, and re-layouts  42.3 us (18%)
  loops' own time  27.4 us (12%)
  matrix products  20.7 us (9%)
  starting transfers between devices  17.2 us (7%)
    ppermute x3, waiting for transfers between devices, partner(): return lax.ppermute(block, axis, route)  34.9 us
    another operation x1, loops' own time, on_device(): lax.scan(advance, initial, jnp.arange(slices, dtype=jnp.int32))  27.4 us
    ppermute x2, waiting for transfers between devices, extended_2(): lax.ppermute(lax.slice_in_dim(block, block.shape[dim] - width, None, axis...  22 us
    dot_general x8, matrix products, advance(): jnp.dot(sheared.reshape(4 * columns, height), interp, preferred_element_t...  20.7 us
    mul x8, other arithmetic, advance(): transmit = transmit * (1.0 - resampled[3])  17.6 us
    another operation x3, other arithmetic, shade_cells(): jnp.stack([red_part, green_part, blue_part, opacity], axis=1)  13.7 us
    slice x8, local copies, waits for them, and re-layouts, advance(): colour_front = colour_front + transmit[None] * resampled[:3]  12.6 us
    dynamic_slice x8, local copies, waits for them, and re-layouts, advance(): lax.dynamic_slice(plane, (anchor, start, anchor), (4, columns, height))  12.1 us
  transfers between devices with their start and end apart: 8, of which 6 were waited for; matrix products, arithmetic and copies ran while one was open for 1% of the time, Pallas kernels for 0%

commit v1 on v0

v1 whole, which is shorter than its diff:
```python
import functools

import jax
import jax.numpy as jnp
from jax import lax
from jax.experimental import pallas as pl
from jax.experimental.pallas import tpu as pltpu
from jax.sharding import PartitionSpec as P

SMAX = 8
LEFT = SMAX + 1
SUB = 8
LANES = 128
MESH = pl.DeviceIdType.MESH
DENSITY_SCALE = 65535.0 / 12.0
IMAGE_SCALE = 65530.0


def pack(low, high):
    return low | lax.shift_left(high, jnp.full_like(high, 16))


def low_half(word):
    return (word & 0xFFFF).astype(jnp.float32)


def high_half(word):
    return lax.shift_right_logical(word, jnp.full_like(word, 16)).astype(jnp.float32)


def density_code(value):
    return ((value + 6.0) * DENSITY_SCALE + 0.5).astype(jnp.int32)


def density_value(code):
    return code * (1.0 / DENSITY_SCALE) - 6.0


def image_code(value):
    root = jnp.sqrt(jnp.sqrt(jnp.sqrt(value)))
    return (root * IMAGE_SCALE + 0.5).astype(jnp.int32)


def image_value(code):
    root = code * (1.0 / IMAGE_SCALE)
    square = root * root
    fourth = square * square
    return fourth * fourth


def kernel(
    col_count, depth_count,
    dens, offsets, flips, weights, out,
    nat, ext, zsend, zrecv, crecv, lhs0, lhs1, res, kept, ysend, yrecv, isend, irecv, final,
    in_sem, col_send, col_recv, z_send, z_recv, c_send, c_recv, y_send, y_recv, i_send, i_recv,
):
    slices, columns, height = nat.shape
    absorb = 0.5 / (slices * depth_count)
    block = columns // depth_count
    pairs = depth_count // 2
    half = columns // 2
    chunk = min(8, block)
    group = min(4, chunk)
    col = lax.axis_index("col")
    depth = lax.axis_index("depth")
    side = lax.rem(depth, 2)
    rank = depth // 2
    has_left, has_right = col > 0, col < col_count - 1
    has_up, has_down = depth > 0, depth < depth_count - 1

    def at(c, d):
        return {"col": c, "depth": d}

    order = [0, slices - 1] + list(range(1, slices - 1))
    loads = [pltpu.make_async_copy(dens.at[k], nat.at[k], in_sem.at[k]) for k in range(slices)]
    for k in order:
        loads[k].start()

    barrier = pltpu.get_barrier_semaphore()

    def greet(c, d):
        pl.semaphore_signal(barrier, inc=1, device_id=at(c, d), device_id_type=MESH)

    def greet_rank(i, carry):
        greet(col, lax.rem(rank + i, pairs) * 2 + side)
        return carry

    lax.fori_loop(1, pairs, greet_rank, 0)
    pl.when(has_up)(lambda: greet(col, depth - 1))
    pl.when(has_down)(lambda: greet(col, depth + 1))
    one = jnp.int32(1)
    none = jnp.int32(0)
    depth_sides = jnp.where(has_up, one, none) + jnp.where(has_down, one, none)
    col_sides = jnp.where(has_left, one, none) + jnp.where(has_right, one, none)
    for step, present in ((-1, has_left), (1, has_right)):
        pl.when(present)(lambda step=step: greet(col + step, depth))
        pl.when(present & has_up)(lambda step=step: greet(col + step, depth - 1))
        pl.when(present & has_down)(lambda step=step: greet(col + step, depth + 1))

    def relayout(k):
        def body(i, carry):
            x0 = pl.multiple_of(i * 8, 8)
            ext[k + 1, pl.ds(LEFT + x0, 8)] = nat[k, pl.ds(x0, 8), :].reshape(8, SUB, LANES)
            return carry

        lax.fori_loop(0, columns // 8, body, 0)

    def encode_slice(slot, k):
        def body(i, carry):
            low = ext[k + 1, pl.ds(LEFT + i * 8, 8)]
            high = ext[k + 1, pl.ds(LEFT + half + i * 8, 8)]
            zsend[slot, pl.ds(i * 8, 8)] = pack(density_code(low), density_code(high))
            return carry

        lax.fori_loop(0, half // 8, body, 0)

    for k in (0, slices - 1):
        loads[k].wait()
        relayout(k)
    encode_slice(0, slices - 1)
    encode_slice(1, 0)
    pl.semaphore_wait(barrier, pairs - 1 + depth_sides + col_sides + col_sides * depth_sides)

    def remote(src, dst, send, recv, c, d):
        return pltpu.make_async_remote_copy(
            src_ref=src, dst_ref=dst, send_sem=send, recv_sem=recv, device_id=at(c, d), device_id_type=MESH
        )

    tail = pl.ds(half - SMAX, SMAX)
    z_copies = [
        remote(zsend.at[0], zrecv.at[0], z_send.at[0], z_recv.at[0], col, depth + 1),
        remote(zsend.at[1], zrecv.at[1], z_send.at[1], z_recv.at[1], col, depth - 1),
    ]
    c_copies = [
        remote(zsend.at[0, tail], crecv.at[0], c_send.at[0], c_recv.at[0], col + 1, depth + 1),
        remote(zsend.at[1, tail], crecv.at[1], c_send.at[1], c_recv.at[1], col + 1, depth - 1),
    ]
    z_out = (has_down, has_up)
    z_in = (has_up, has_down)
    for slot in range(2):
        pl.when(z_out[slot])(z_copies[slot].start)
        pl.when(z_out[slot] & has_right)(c_copies[slot].start)

    for k in range(1, slices - 1):
        loads[k].wait()
        relayout(k)
    inner = pl.ds(1, slices)
    to_right = remote(
        ext.at[inner, pl.ds(columns, LEFT)], ext.at[inner, pl.ds(0, LEFT)],
        col_send.at[0], col_recv.at[0], col + 1, depth,
    )
    to_left = remote(
        ext.at[inner, pl.ds(LEFT, 1)], ext.at[inner, pl.ds(LEFT + columns, 1)],
        col_send.at[1], col_recv.at[1], col - 1, depth,
    )
    pl.when(has_right)(to_right.start)
    pl.when(has_left)(to_left.start)

    @pl.when(jnp.logical_not(has_left))
    def _():
        ext[:, pl.ds(0, LEFT)] = jnp.zeros((slices + 2, LEFT, SUB, LANES), jnp.float32)

    @pl.when(jnp.logical_not(has_right))
    def _():
        ext[:, pl.ds(LEFT + columns, 1)] = jnp.zeros((slices + 2, 1, SUB, LANES), jnp.float32)

    def wait_col():
        pl.when(has_right)(to_right.wait_send)
        pl.when(has_left)(to_left.wait_send)
        pl.when(has_left)(to_right.wait_recv)
        pl.when(has_right)(to_left.wait_recv)

    wait_col()

    shape = (group, SUB, LANES)
    lane = lax.broadcasted_iota(jnp.int32, shape, 2)
    sub = lax.broadcasted_iota(jnp.int32, shape, 1)
    not_first = jnp.where(sub == 0, 0.0, 1.0)
    not_last = jnp.where(sub == SUB - 1, 0.0, 1.0)
    low_lanes = lane < LANES // 2
    edge_mask = jnp.where(low_lanes, not_last, not_first)

    def shade(k, x0, lhs):
        for g in range(chunk // group):
            row = LEFT + x0 + g * group - offsets[k]
            rows = group * SUB
            window = [ext[k + 1, row + i] for i in range(-1, group + 1)]
            center = jnp.stack(window[1:-1])
            dx = jnp.stack(window[2:]) - jnp.stack(window[:-2])
            dz = jnp.stack([ext[k + 2, row + i] - ext[k, row + i] for i in range(group)])
            before = jnp.where(lane == LANES - 1, pltpu.roll(center, 1, 1) * not_first, center)
            after = jnp.where(lane == 0, pltpu.roll(center, SUB - 1, 1) * not_last, center)
            dy = pltpu.roll(after, LANES - 1, 2) - pltpu.roll(before, 1, 2)
            square = dx * dx + dy * dy + dz * dz
            lambert = (0.48 * dx + 0.6 * dy + 0.64 * dz) * lax.rsqrt(jnp.maximum(square, 4.0))
            center_sq = center * center
            opacity = 1.0 - jnp.exp(-absorb * center_sq * center_sq)
            halved = opacity * (0.1 + 0.4 * jnp.abs(lambert))
            tilt = halved * jnp.tanh(center)
            green = halved + halved * jnp.tanh(0.5 - 0.5 * center_sq)
            for ch, value in enumerate((halved + tilt, green, halved - tilt, opacity)):
                edge = jnp.where(low_lanes, pltpu.roll(value, SUB - 1, 1), pltpu.roll(value, 1, 1)) * edge_mask
                place = pl.ds((ch * chunk + g * group) * SUB, rows)
                lhs[place, 0:LANES] = value.reshape(rows, LANES).astype(jnp.bfloat16)
                lhs[place, LANES : 2 * LANES] = edge.reshape(rows, LANES).astype(jnp.bfloat16)

    def resample(k, x0, lhs):
        value = jnp.dot(lhs[...], weights[...], preferred_element_type=jnp.float32)
        res[k, :, pl.ds(x0, chunk)] = value.reshape(4, chunk, SUB, LANES)

    def inner_slice(k, carry):
        def body(i, inner_carry):
            x0 = i * 2 * chunk
            shade(k, x0, lhs0)
            resample(k, x0, lhs0)
            shade(k, x0 + chunk, lhs1)
            resample(k, x0 + chunk, lhs1)
            return inner_carry

        return lax.fori_loop(0, columns // (2 * chunk), body, carry)

    lax.fori_loop(1, slices - 1, inner_slice, 0)

    def decode_slice(slot, plane):
        def body(i, carry):
            word = zrecv[slot, pl.ds(i * 8, 8)]
            ext[plane, pl.ds(LEFT + i * 8, 8)] = density_value(low_half(word))
            ext[plane, pl.ds(LEFT + half + i * 8, 8)] = density_value(high_half(word))
            return carry

        lax.fori_loop(0, half // 8, body, 0)

    for slot, plane in ((0, 0), (1, slices + 1)):
        @pl.when(z_in[slot])
        def _(slot=slot, plane=plane):
            z_copies[slot].wait_recv()
            decode_slice(slot, plane)

        @pl.when(z_in[slot] & has_left)
        def _(slot=slot, plane=plane):
            c_copies[slot].wait_recv()
            ext[plane, pl.ds(1, SMAX)] = density_value(high_half(crecv[slot]))

        @pl.when(jnp.logical_not(z_in[slot]))
        def _(plane=plane):
            ext[plane] = jnp.zeros(ext.shape[1:], jnp.float32)

    def finish_block(number):
        start = number * block
        for i in range(block // chunk):
            shade(0, start + i * chunk, lhs0)
            resample(0, start + i * chunk, lhs0)
            shade(slices - 1, start + i * chunk, lhs1)
            resample(slices - 1, start + i * chunk, lhs1)

    def column_partial(x):
        flip = flips[x]
        colour = [None] * 3
        transmit = None
        for i in range(slices):
            k = i + flip * (slices - 1 - 2 * i)
            through = 1.0 - res[k, 3, x]
            for ch in range(3):
                value = res[k, ch, x]
                colour[ch] = value if i == 0 else colour[ch] + transmit * value
            transmit = through if i == 0 else transmit * through
        return colour, transmit

    def store_codes(ref, slot, x, colour, opacity):
        ref[slot, 0, x] = pack(image_code(colour[0]), image_code(colour[1]))
        ref[slot, 1, x] = pack(image_code(colour[2]), image_code(opacity))

    def load_codes(first, second):
        colour = [image_value(low_half(first)), image_value(high_half(first)), image_value(low_half(second))]
        return colour, image_value(high_half(second))

    def y_copy(slot):
        return remote(ysend.at[slot], yrecv.at[slot], y_send.at[slot], y_recv.at[slot], col, depth + 1 - 2 * side)

    def i_copy(slot):
        return remote(isend.at[slot], irecv.at[rank], i_send.at[slot], i_recv.at[rank], col, 2 * slot + side)

    def give(i, carry):
        slot = lax.rem(rank + 1 + i, pairs)
        number = 2 * slot + 1 - side
        finish_block(number)

        def body(x, inner_carry):
            colour, transmit = column_partial(number * block + x)
            store_codes(ysend, slot, x, colour, 1.0 - transmit)
            return inner_carry

        lax.fori_loop(0, block, body, 0)
        y_copy(slot).start()
        return carry

    lax.fori_loop(0, pairs, give, 0)

    def keep(i, carry):
        slot = lax.rem(rank + 1 + i, pairs)
        number = 2 * slot + side
        finish_block(number)

        def body(x, inner_carry):
            colour, transmit = column_partial(number * block + x)
            for ch in range(3):
                kept[ch, x] = colour[ch]
            kept[3, x] = transmit
            return inner_carry

        lax.fori_loop(0, block, body, 0)
        y_copy(slot).wait_recv()

        def join(x, inner_carry):
            theirs, their_opacity = load_codes(yrecv[slot, 0, x], yrecv[slot, 1, x])
            their_transmit = 1.0 - their_opacity
            mine = [kept[ch, x] for ch in range(3)]
            my_transmit = kept[3, x]
            mine_first = jnp.full((SUB, LANES), flips[number * block + x], jnp.int32) == side
            front_transmit = jnp.where(mine_first, my_transmit, their_transmit)
            colour = []
            for ch in range(3):
                front = jnp.where(mine_first, mine[ch], theirs[ch])
                behind = jnp.where(mine_first, theirs[ch], mine[ch])
                colour.append(front + front_transmit * behind)
            opacity = 1.0 - my_transmit * their_transmit

            @pl.when(i < pairs - 1)
            def _():
                store_codes(isend, slot, x, colour, opacity)

            @pl.when(i == pairs - 1)
            def _():
                store_codes(irecv, rank, x, colour, opacity)

            return inner_carry

        lax.fori_loop(0, block, join, 0)
        pl.when(i < pairs - 1)(lambda: i_copy(slot).start())
        return carry

    lax.fori_loop(0, pairs, keep, 0)

    def arrive(i, carry):
        slot = lax.rem(rank + i, pairs)
        remote(
            isend.at[slot], irecv.at[slot], i_send.at[slot], i_recv.at[slot], col, 2 * slot + side
        ).wait_recv()
        return carry

    lax.fori_loop(1, pairs, arrive, 0)

    def compose(x, carry):
        flip = flips[depth * block + x]
        colour = [None] * 3
        transmit = None
        for i in range(pairs):
            slot = i + flip * (pairs - 1 - 2 * i)
            value, opacity = load_codes(irecv[slot, 0, x], irecv[slot, 1, x])
            for ch in range(3):
                colour[ch] = value[ch] if i == 0 else colour[ch] + transmit * value[ch]
            transmit = 1.0 - opacity if i == 0 else transmit * (1.0 - opacity)
        for ch in range(3):
            final[ch, x] = colour[ch]
        final[3, x] = 1.0 - transmit
        return carry

    lax.fori_loop(0, block, compose, 0)
    part = min(8, block)
    for ch in range(4):
        for x0 in range(0, block, part):
            out[ch, x0 : x0 + part, :] = final[ch, x0 : x0 + part].reshape(part, height)

    for slot in range(2):
        pl.when(z_out[slot])(z_copies[slot].wait_send)
        pl.when(z_out[slot] & has_right)(c_copies[slot].wait_send)

    def left_y(i, carry):
        y_copy(i).wait_send()
        return carry

    lax.fori_loop(0, pairs, left_y, 0)

    def left_i(i, carry):
        i_copy(lax.rem(rank + i, pairs)).wait_send()
        return carry

    lax.fori_loop(1, pairs, left_i, 0)


def resample_weights():
    source = jnp.arange(LANES, dtype=jnp.int32)[:, None]
    target = jnp.arange(LANES, dtype=jnp.int32)[None, :]

    def taps(distance):
        distance = jnp.abs(distance)
        return jnp.where(distance == 0, 0.5, jnp.where(distance == 1, 0.1875, jnp.where(distance == 2, 0.0625, 0.0)))

    own = taps(source - target)
    beside = jnp.where(source < LANES // 2, taps(source + LANES - target), taps(source - LANES - target))
    return jnp.concatenate([own, beside], axis=0).astype(jnp.bfloat16)


def on_device(density, offsets, view_flip):
    col_count, depth_count = lax.axis_size("col"), lax.axis_size("depth")
    slices, columns, height = density.shape
    block = columns // depth_count
    pairs = depth_count // 2
    chunk = min(8, block)
    half = columns // 2
    f32, i32 = jnp.float32, jnp.int32
    dma = pltpu.SemaphoreType.DMA
    image = pltpu.VMEM((pairs, 2, block, SUB, LANES), i32)
    scratch = [
        pltpu.VMEM((slices, columns, height), f32),
        pltpu.VMEM((slices + 2, LEFT + columns + 1, SUB, LANES), f32),
        pltpu.VMEM((2, half, SUB, LANES), i32),
        pltpu.VMEM((2, half, SUB, LANES), i32),
        pltpu.VMEM((2, SMAX, SUB, LANES), i32),
        pltpu.VMEM((4 * chunk * SUB, 2 * LANES), jnp.bfloat16),
        pltpu.VMEM((4 * chunk * SUB, 2 * LANES), jnp.bfloat16),
        pltpu.VMEM((slices, 4, columns, SUB, LANES), f32),
        pltpu.VMEM((4, block, SUB, LANES), f32),
        image, image, image, image,
        pltpu.VMEM((4, block, SUB, LANES), f32),
        dma((slices,)),
        dma((2,)), dma((2,)), dma((2,)), dma((2,)), dma((2,)), dma((2,)),
        dma((pairs,)), dma((pairs,)), dma((pairs,)), dma((pairs,)),
    ]
    vmem = pl.BlockSpec(memory_space=pltpu.VMEM)
    smem = pl.BlockSpec(memory_space=pltpu.SMEM)
    return pl.pallas_call(
        functools.partial(kernel, col_count, depth_count),
        out_shape=jax.ShapeDtypeStruct((4, block, height), f32),
        in_specs=[pl.BlockSpec(memory_space=pl.ANY), smem, smem, vmem],
        out_specs=vmem,
        scratch_shapes=scratch,
        compiler_params=pltpu.CompilerParams(
            collective_id=0, has_side_effects=True, vmem_limit_bytes=48 * 2**20
        ),
    )(density, offsets, view_flip, resample_weights())


def solution(mesh):
    in_specs = (P("depth", "col", None), P("depth"), P("col"))
    out_specs = P(None, ("col", "depth"), None)
    return jax.shard_map(
        on_device, mesh=mesh, in_specs=in_specs, out_specs=out_specs, check_vma=False
    )
```

time: 232 us -> 50.7 us (0.22); the launches traced: 228 us -> 49.7 us
  waiting for transfers between devices: 65.7 us -> 0 us
  other arithmetic: 54.2 us -> 0.17 us
  Pallas kernels: 0 us -> 45.3 us
  local copies, waits for them, and re-layouts: 42.3 us -> 4.2 us
  loops' own time: 27.4 us -> 0 us
  matrix products: 20.7 us -> 0 us
  starting transfers between devices: 17.2 us -> 0 us
    ppermute x8 -> x0, waiting for transfers between devices: 65.7 us -> none  [the longest x3 34.9 us: partner(): return lax.ppermute(block, axis, route)]
    pallas_call x0 -> x1, Pallas kernels: none -> 45.3 us  [on_device(): pl.pallas_call(functools.partial(kernel, col_count, depth_count), out_sha...]
    another operation x1 -> x0, loops' own time: 27.4 us -> none  [on_device(): lax.scan(advance, initial, jnp.arange(slices, dtype=jnp.int32))]
    dynamic_slice x24 -> x0, local copies, waits for them, and re-layouts: 22.5 us -> none  [the longest x8 12.1 us: advance(): lax.dynamic_slice(plane, (anchor, start, anchor), (4, columns, height))]
    dot_general x8 -> x0, matrix products: 20.7 us -> none  [advance(): jnp.dot(sheared.reshape(4 * columns, height), interp, preferred_element_t...]
    mul x11 -> x0, other arithmetic: 17.6 us -> none  [the longest x8 17.6 us: advance(): transmit = transmit * (1.0 - resampled[3])]
    ppermute x8 -> x0, starting transfers between devices: 17.2 us -> none  [the longest x2 5.83 us: extended_2(): lax.ppermute(lax.slice_in_dim(block, block.shape[dim] - width, None, axis...]
    slice x10 -> x0, local copies, waits for them, and re-layouts: 13.9 us -> none  [the longest x8 12.6 us: advance(): colour_front = colour_front + transmit[None] * resampled[:3]]
  transfers between devices with their start and end apart: 8 -> 0, of which waited for: 6 -> 0; matrix products, arithmetic and copies ran while one was open for 1% -> 0% of each run, Pallas kernels for 0% -> 0%
where the time goes in v1:
time: 50.7 us; the launch traced here: 49.7 us
  Pallas kernels  45.3 us (89%)
  local copies, waits for them, and re-layouts  4.2 us (8%)
    pallas_call x1, Pallas kernels, on_device(): pl.pallas_call(functools.partial(kernel, col_count, depth_count), out_sha...  45.3 us
    unnamed x7, local copies, waits for them, and re-layouts  4.2 us

profile of v1, /device:TPU:10, one launch (start us, length us, event | category | flops | bytes accessed | tf_op | source)
XLA Modules:
  0.0 49.7 jit_solution(555030158545926378)
XLA Ops:
  0.0 0.1 select_convert_fusion
  0.2 0.0 copy-start
  0.2 2.2 %copy-done = f32[8,128,1024]{2,1,0:T(8,128)S(1)} copy-done((f32[8,128,1024]{2,1,0:T(8,128)S(1)}, f32[8,128,1024]{2,1,0:T(8,128)}, u32[]{:S(2)}) %copy-start) | copy-done | bytes 4194328
  2.4 0.0 copy-start.1
  2.4 0.7 %copy-done.1 = s32[8]{0:T(128)S(1)} copy-done((s32[8]{0:T(128)S(1)}, s32[8]{0:T(128)}, u32[]{:S(2)}) %copy-start.1) | copy-done | bytes 56
  3.0 0.0 copy-start.2
  3.0 0.7 %copy-done.2 = s32[128]{0:T(128)S(1)} copy-done((s32[128]{0:T(128)S(1)}, s32[128]{0:T(128)}, u32[]{:S(2)}) %copy-start.2) | copy-done | bytes 536
  3.7 45.3 %shard_map.37 = f32[4,16,1024]{2,1,0:T(8,128)S(1)} custom-call(f32[8,128,1024]{2,1,0:T(8,128)S(1)} %copy-done, s32[8]{0:T(128)S(1)} %copy-done.1, s32[128]{0:T(128)S(1)} %copy-done.2, bf16[256,128]{1,0:T(8,128)(2,1)S(1)} %pad_maximum_fusion.weights), custom_call_target="tpu_custom_call" | custom-call | tf_op jit(solution)/shard_map/pallas_call | solution.py:432
  49.0 0.7 %copy.5 = f32[4,16,1024]{2,1,0:T(8,128)} copy(f32[4,16,1024]{2,1,0:T(8,128)S(1)} %shard_map.37) | data formatting | bytes 524288
  (4 shorter events, 0.0 us)
Async XLA Ops:
  0.2 2.2 %copy-start = (f32[8,128,1024]{2,1,0:T(8,128)S(1)}, f32[8,128,1024]{2,1,0:T(8,128)}, u32[]{:S(2)}) copy-start(f32[8,128,1024]{2,1,0:T(8,128)} %dens.1) | copy-start | bytes 12582916
  2.4 0.7 %copy-start.1 = (s32[8]{0:T(128)S(1)}, s32[8]{0:T(128)}, u32[]{:S(2)}) copy-start(s32[8]{0:T(128)} %offsets.1) | copy-start | bytes 100
  3.0 0.7 %copy-start.2 = (s32[128]{0:T(128)S(1)}, s32[128]{0:T(128)}, u32[]{:S(2)}) copy-start(s32[128]{0:T(128)} %flips.1) | copy-start | bytes 1540

commit v2 on v1

--- a/solution.py
+++ b/solution.py
@@ -50,17 +50,18 @@
 
 def kernel(
     col_count, depth_count,
-    dens, offsets, flips, weights, out,
-    nat, ext, zsend, zrecv, crecv, lhs0, lhs1, res, kept, ysend, yrecv, isend, irecv, final,
-    in_sem, col_send, col_recv, z_send, z_recv, c_send, c_recv, y_send, y_recv, i_send, i_recv,
+    dens, offsets_in, flips_in, out,
+    offsets, flips, weights, nat, ext, lrecv, rrecv, zsend, zrecv, crecv, lhs0, lhs1, res, kept,
+    ysend, yrecv, isend, irecv, final, small_sem, in_sem, col_send, col_recv, z_send, z_recv, c_send, c_recv, y_send, y_recv, i_send, i_recv,
 ):
     slices, columns, height = nat.shape
     absorb = 0.5 / (slices * depth_count)
     block = columns // depth_count
     pairs = depth_count // 2
     half = columns // 2
-    chunk = min(8, block)
+    chunk = min(16, block)
     group = min(4, chunk)
+    lump = min(4, block)
     col = lax.axis_index("col")
     depth = lax.axis_index("depth")
     side = lax.rem(depth, 2)
@@ -75,6 +76,13 @@
     loads = [pltpu.make_async_copy(dens.at[k], nat.at[k], in_sem.at[k]) for k in range(slices)]
     for k in order:
         loads[k].start()
+
+    small = [
+        pltpu.make_async_copy(offsets_in, offsets, small_sem.at[0]),
+        pltpu.make_async_copy(flips_in, flips, small_sem.at[1]),
+    ]
+    for load in small:
+        load.start()
 
     barrier = pltpu.get_barrier_semaphore()
 
@@ -97,13 +105,16 @@
         pl.when(present & has_up)(lambda step=step: greet(col + step, depth - 1))
         pl.when(present & has_down)(lambda step=step: greet(col + step, depth + 1))
 
+    def move(k, x0):
+        ext[k + 1, pl.ds(LEFT + x0, 8)] = nat[k, pl.ds(x0, 8), :].reshape(8, SUB, LANES)
+
     def relayout(k):
         def body(i, carry):
-            x0 = pl.multiple_of(i * 8, 8)
-            ext[k + 1, pl.ds(LEFT + x0, 8)] = nat[k, pl.ds(x0, 8), :].reshape(8, SUB, LANES)
+            for u in range(4):
+                move(k, pl.multiple_of(i * 32 + u * 8, 8))
             return carry
 
-        lax.fori_loop(0, columns // 8, body, 0)
+        lax.fori_loop(0, columns // 32, body, 0)
 
     def encode_slice(slot, k):
         def body(i, carry):
@@ -143,34 +154,36 @@
 
     for k in range(1, slices - 1):
         loads[k].wait()
-        relayout(k)
+        for x0 in (0, columns - 16, columns - 8):
+            move(k, x0)
     inner = pl.ds(1, slices)
-    to_right = remote(
-        ext.at[inner, pl.ds(columns, LEFT)], ext.at[inner, pl.ds(0, LEFT)],
-        col_send.at[0], col_recv.at[0], col + 1, depth,
-    )
-    to_left = remote(
-        ext.at[inner, pl.ds(LEFT, 1)], ext.at[inner, pl.ds(LEFT + columns, 1)],
-        col_send.at[1], col_recv.at[1], col - 1, depth,
-    )
+    to_right = remote(ext.at[inner, pl.ds(columns, LEFT)], lrecv, col_send.at[0], col_recv.at[0], col + 1, depth)
+    to_left = remote(ext.at[inner, pl.ds(LEFT, 1)], rrecv, col_send.at[1], col_recv.at[1], col - 1, depth)
     pl.when(has_right)(to_right.start)
     pl.when(has_left)(to_left.start)
 
-    @pl.when(jnp.logical_not(has_left))
-    def _():
-        ext[:, pl.ds(0, LEFT)] = jnp.zeros((slices + 2, LEFT, SUB, LANES), jnp.float32)
-
-    @pl.when(jnp.logical_not(has_right))
-    def _():
-        ext[:, pl.ds(LEFT + columns, 1)] = jnp.zeros((slices + 2, 1, SUB, LANES), jnp.float32)
-
-    def wait_col():
-        pl.when(has_right)(to_right.wait_send)
-        pl.when(has_left)(to_left.wait_send)
-        pl.when(has_left)(to_right.wait_recv)
-        pl.when(has_right)(to_left.wait_recv)
-
-    wait_col()
+    def relayout_inner(k, carry):
+        def body(i, inner_carry):
+            for u in range(4):
+                move(k, pl.multiple_of(8 + jnp.minimum(i * 32 + u * 8, columns - 32), 8))
+            return inner_carry
+
+        return lax.fori_loop(0, columns // 32, body, carry)
+
+    lax.fori_loop(1, slices - 1, relayout_inner, 0)
+
+    source = lax.broadcasted_iota(jnp.int32, (LANES, LANES), 0)
+    target = lax.broadcasted_iota(jnp.int32, (LANES, LANES), 1)
+
+    def taps(distance):
+        distance = jnp.abs(distance)
+        return jnp.where(distance == 0, 0.5, jnp.where(distance == 1, 0.1875, jnp.where(distance == 2, 0.0625, 0.0)))
+
+    weights[0:LANES, :] = taps(source - target).astype(jnp.bfloat16)
+    shift = jnp.where(source < LANES // 2, LANES, -LANES)
+    weights[LANES : 2 * LANES, :] = taps(source + shift - target).astype(jnp.bfloat16)
+    for load in small:
+        load.wait()
 
     shape = (group, SUB, LANES)
     lane = lax.broadcasted_iota(jnp.int32, shape, 2)
@@ -208,18 +221,61 @@
         value = jnp.dot(lhs[...], weights[...], preferred_element_type=jnp.float32)
         res[k, :, pl.ds(x0, chunk)] = value.reshape(4, chunk, SUB, LANES)
 
-    def inner_slice(k, carry):
-        def body(i, inner_carry):
-            x0 = i * 2 * chunk
-            shade(k, x0, lhs0)
-            resample(k, x0, lhs0)
-            shade(k, x0 + chunk, lhs1)
-            resample(k, x0 + chunk, lhs1)
-            return inner_carry
-
-        return lax.fori_loop(0, columns // (2 * chunk), body, carry)
-
-    lax.fori_loop(1, slices - 1, inner_slice, 0)
+    def run(count, place):
+        shade(*place(0), lhs0)
+
+        def pair(i, last):
+            resample(*place(2 * i), lhs0)
+            shade(*place(2 * i + 1), lhs1)
+            resample(*place(2 * i + 1), lhs1)
+            if not last:
+                shade(*place(2 * i + 2), lhs0)
+
+        def body(i, carry):
+            pair(i, False)
+            return carry
+
+        lax.fori_loop(0, count // 2 - 1, body, 0)
+        pair(count // 2 - 1, True)
+
+    chunks = columns // chunk
+    left_chunks = -(-LEFT // chunk)
+    mid_chunks = chunks - left_chunks - 1
+    rim_chunks = left_chunks + 1
+    mid_slices = slices - 2
+
+    def mid_place(t):
+        t = jnp.int32(t)
+        return 1 + t // mid_chunks, (left_chunks + lax.rem(t, mid_chunks)) * chunk
+
+    def rim_place(t):
+        t = jnp.int32(t)
+        return 1 + t // rim_chunks, lax.rem(chunks - 1 + lax.rem(t, rim_chunks), chunks) * chunk
+
+    run(mid_slices * mid_chunks, mid_place)
+
+    pl.when(has_right)(to_right.wait_send)
+    pl.when(has_left)(to_left.wait_send)
+
+    @pl.when(has_left)
+    def _():
+        to_right.wait_recv()
+        ext[1 : slices + 1, 0:LEFT] = lrecv[...]
+
+    @pl.when(has_right)
+    def _():
+        to_left.wait_recv()
+        ext[1 : slices + 1, LEFT + columns : LEFT + columns + 1] = rrecv[...]
+
+    @pl.when(jnp.logical_not(has_left))
+    def _():
+        ext[:, 0:LEFT] = jnp.zeros((slices + 2, LEFT, SUB, LANES), jnp.float32)
+
+    @pl.when(jnp.logical_not(has_right))
+    def _():
+        ext[:, LEFT + columns : LEFT + columns + 1] = jnp.zeros((slices + 2, 1, SUB, LANES), jnp.float32)
+
+    run(mid_slices * rim_chunks, rim_place)
 
     def decode_slice(slot, plane):
         def body(i, carry):
@@ -254,21 +310,22 @@
             resample(slices - 1, start + i * chunk, lhs1)
 
     def column_partial(x):
-        flip = flips[x]
+        flip = [flips[x + u] for u in range(lump)]
         colour = [None] * 3
         transmit = None
         for i in range(slices):
-            k = i + flip * (slices - 1 - 2 * i)
-            through = 1.0 - res[k, 3, x]
+            depths = [i + flip[u] * (slices - 1 - 2 * i) for u in range(lump)]
+            through = 1.0 - jnp.stack([res[depths[u], 3, x + u] for u in range(lump)])
             for ch in range(3):
-                value = res[k, ch, x]
+                value = jnp.stack([res[depths[u], ch, x + u] for u in range(lump)])
                 colour[ch] = value if i == 0 else colour[ch] + transmit * value
             transmit = through if i == 0 else transmit * through
         return colour, transmit
 
     def store_codes(ref, slot, x, colour, opacity):
-        ref[slot, 0, x] = pack(image_code(colour[0]), image_code(colour[1]))
-        ref[slot, 1, x] = pack(image_code(colour[2]), image_code(opacity))
+        span = pl.ds(x, lump)
+        ref[slot, 0, span] = pack(image_code(colour[0]), image_code(colour[1]))
+        ref[slot, 1, span] = pack(image_code(colour[2]), image_code(opacity))
 
     def load_codes(first, second):
         colour = [image_value(low_half(first)), image_value(high_half(first)), image_value(low_half(second))]
@@ -285,12 +342,13 @@
         number = 2 * slot + 1 - side
         finish_block(number)
 
-        def body(x, inner_carry):
+        def body(step, inner_carry):
+            x = step * lump
             colour, transmit = column_partial(number * block + x)
             store_codes(ysend, slot, x, colour, 1.0 - transmit)
             return inner_carry
 
-        lax.fori_loop(0, block, body, 0)
+        lax.fori_loop(0, block // lump, body, 0)
         y_copy(slot).start()
         return carry
 
@@ -301,22 +359,26 @@
         number = 2 * slot + side
         finish_block(number)
 
-        def body(x, inner_carry):
+        def body(step, inner_carry):
+            x = step * lump
             colour, transmit = column_partial(number * block + x)
             for ch in range(3):
-                kept[ch, x] = colour[ch]
-            kept[3, x] = transmit
+                kept[ch, pl.ds(x, lump)] = colour[ch]
+            kept[3, pl.ds(x, lump)] = transmit
             return inner_carry
 
-        lax.fori_loop(0, block, body, 0)
+        lax.fori_loop(0, block // lump, body, 0)
         y_copy(slot).wait_recv()
 
-        def join(x, inner_carry):
-            theirs, their_opacity = load_codes(yrecv[slot, 0, x], yrecv[slot, 1, x])
+        def join(step, inner_carry):
+            x = step * lump
+            span = pl.ds(x, lump)
+            theirs, their_opacity = load_codes(yrecv[slot, 0, span], yrecv[slot, 1, span])
             their_transmit = 1.0 - their_opacity
-            mine = [kept[ch, x] for ch in range(3)]
-            my_transmit = kept[3, x]
-            mine_first = jnp.full((SUB, LANES), flips[number * block + x], jnp.int32) == side
+            mine = [kept[ch, span] for ch in range(3)]
+            my_transmit = kept[3, span]
+            flip = [jnp.full((SUB, LANES), flips[number * block + x + u], jnp.int32) for u in range(lump)]
+            mine_first = jnp.stack(flip) == side
             front_transmit = jnp.where(mine_first, my_transmit, their_transmit)
             colour = []
             for ch in range(3):
@@ -335,7 +397,7 @@
 
             return inner_carry
 
-        lax.fori_loop(0, block, join, 0)
+        lax.fori_loop(0, block // lump, join, 0)
         pl.when(i < pairs - 1)(lambda: i_copy(slot).start())
         return carry
 
@@ -350,22 +412,24 @@
 
     lax.fori_loop(1, pairs, arrive, 0)
 
-    def compose(x, carry):
-        flip = flips[depth * block + x]
+    def compose(step, carry):
+        x = step * lump
+        flip = [flips[depth * block + x + u] for u in range(lump)]
         colour = [None] * 3
         transmit = None
         for i in range(pairs):
-            slot = i + flip * (pairs - 1 - 2 * i)
-            value, opacity = load_codes(irecv[slot, 0, x], irecv[slot, 1, x])
+            slot = [i + flip[u] * (pairs - 1 - 2 * i) for u in range(lump)]
+            words = [jnp.stack([irecv[slot[u], part, x + u] for u in range(lump)]) for part in range(2)]
+            value, opacity = load_codes(*words)
             for ch in range(3):
                 colour[ch] = value[ch] if i == 0 else colour[ch] + transmit * value[ch]
             transmit = 1.0 - opacity if i == 0 else transmit * (1.0 - opacity)
         for ch in range(3):
-            final[ch, x] = colour[ch]
-        final[3, x] = 1.0 - transmit
-        return carry
-
-    lax.fori_loop(0, block, compose, 0)
+            final[ch, pl.ds(x, lump)] = colour[ch]
+        final[3, pl.ds(x, lump)] = 1.0 - transmit
+        return carry
+
+    lax.fori_loop(0, block // lump, compose, 0)
     part = min(8, block)
     for ch in range(4):
         for x0 in range(0, block, part):
@@ -386,19 +450,6 @@
         return carry
 
     lax.fori_loop(1, pairs, left_i, 0)
-
-
-def resample_weights():
-    source = jnp.arange(LANES, dtype=jnp.int32)[:, None]
-    target = jnp.arange(LANES, dtype=jnp.int32)[None, :]
-
-    def taps(distance):
-        distance = jnp.abs(distance)
-        return jnp.where(distance == 0, 0.5, jnp.where(distance == 1, 0.1875, jnp.where(distance == 2, 0.0625, 0.0)))
-
-    own = taps(source - target)
-    beside = jnp.where(source < LANES // 2, taps(source + LANES - target), taps(source - LANES - target))
-    return jnp.concatenate([own, beside], axis=0).astype(jnp.bfloat16)
 
 
 def on_device(density, offsets, view_flip):
@@ -406,14 +457,19 @@
     slices, columns, height = density.shape
     block = columns // depth_count
     pairs = depth_count // 2
-    chunk = min(8, block)
+    chunk = min(16, block)
     half = columns // 2
     f32, i32 = jnp.float32, jnp.int32
     dma = pltpu.SemaphoreType.DMA
     image = pltpu.VMEM((pairs, 2, block, SUB, LANES), i32)
     scratch = [
+        pltpu.SMEM((slices,), i32),
+        pltpu.SMEM((columns,), i32),
+        pltpu.VMEM((2 * LANES, LANES), jnp.bfloat16),
         pltpu.VMEM((slices, columns, height), f32),
         pltpu.VMEM((slices + 2, LEFT + columns + 1, SUB, LANES), f32),
+        pltpu.VMEM((slices, LEFT, SUB, LANES), f32),
+        pltpu.VMEM((slices, 1, SUB, LANES), f32),
         pltpu.VMEM((2, half, SUB, LANES), i32),
         pltpu.VMEM((2, half, SUB, LANES), i32),
         pltpu.VMEM((2, SMAX, SUB, LANES), i32),
@@ -423,22 +479,23 @@
         pltpu.VMEM((4, block, SUB, LANES), f32),
         image, image, image, image,
         pltpu.VMEM((4, block, SUB, LANES), f32),
+        dma((2,)),
         dma((slices,)),
         dma((2,)), dma((2,)), dma((2,)), dma((2,)), dma((2,)), dma((2,)),
         dma((pairs,)), dma((pairs,)), dma((pairs,)), dma((pairs,)),
     ]
     vmem = pl.BlockSpec(memory_space=pltpu.VMEM)
-    smem = pl.BlockSpec(memory_space=pltpu.SMEM)
+    hbm = pl.BlockSpec(memory_space=pltpu.HBM)
     return pl.pallas_call(
         functools.partial(kernel, col_count, depth_count),
         out_shape=jax.ShapeDtypeStruct((4, block, height), f32),
-        in_specs=[pl.BlockSpec(memory_space=pl.ANY), smem, smem, vmem],
+        in_specs=[hbm, hbm, hbm],
         out_specs=vmem,
         scratch_shapes=scratch,
         compiler_params=pltpu.CompilerParams(
             collective_id=0, has_side_effects=True, vmem_limit_bytes=48 * 2**20
         ),
-    )(density, offsets, view_flip, resample_weights())
+    )(density, offsets, view_flip)
 
 
 def solution(mesh):

time: 50.7 us -> 42.4 us (0.84)
  the two profiles are of different devices: /device:TPU:10 before, /device:TPU:0 now
where the time goes in v2:
time: 42.4 us; the launch traced here: 42.3 us
  Pallas kernels  38.1 us (90%)
  local copies, waits for them, and re-layouts  4.2 us (10%)
    pallas_call x1, Pallas kernels, on_device(): pl.pallas_call(functools.partial(kernel, col_count, depth_count), out_sha...  38.1 us
    unnamed x7, local copies, waits for them, and re-layouts  4.2 us

profile of v2, /device:TPU:0, one launch (start us, length us, event | category | flops | bytes accessed | tf_op | source)
XLA Modules:
  0.0 42.3 jit_solution(9516642799944646978)
XLA Ops:
  0.0 0.0 copy-start
  0.0 2.2 %copy-done = f32[8,128,1024]{2,1,0:T(8,128)S(1)} copy-done((f32[8,128,1024]{2,1,0:T(8,128)S(1)}, f32[8,128,1024]{2,1,0:T(8,128)}, u32[]{:S(2)}) %copy-start) | copy-done | bytes 4194328
  2.2 0.0 copy-start.1
  2.2 0.7 %copy-done.1 = s32[8]{0:T(128)S(1)} copy-done((s32[8]{0:T(128)S(1)}, s32[8]{0:T(128)}, u32[]{:S(2)}) %copy-start.1) | copy-done | bytes 56
  2.8 0.0 copy-start.2
  2.8 0.7 %copy-done.2 = s32[128]{0:T(128)S(1)} copy-done((s32[128]{0:T(128)S(1)}, s32[128]{0:T(128)}, u32[]{:S(2)}) %copy-start.2) | copy-done | bytes 536
  3.5 38.1 %shard_map.37 = f32[4,16,1024]{2,1,0:T(8,128)S(1)} custom-call(f32[8,128,1024]{2,1,0:T(8,128)S(1)} %copy-done, s32[8]{0:T(128)S(1)} %copy-done.1, s32[128]{0:T(128)S(1)} %copy-done.2), custom_call_target="tpu_custom_call" | custom-call | tf_op jit(solution)/shard_map/pallas_call | solution.py:489
  41.6 0.7 %copy.5 = f32[4,16,1024]{2,1,0:T(8,128)} copy(f32[4,16,1024]{2,1,0:T(8,128)S(1)} %shard_map.37) | data formatting | bytes 524288
Async XLA Ops:
  0.0 2.2 %copy-start = (f32[8,128,1024]{2,1,0:T(8,128)S(1)}, f32[8,128,1024]{2,1,0:T(8,128)}, u32[]{:S(2)}) copy-start(f32[8,128,1024]{2,1,0:T(8,128)} %dens.1) | copy-start | bytes 12582916
  2.2 0.7 %copy-start.1 = (s32[8]{0:T(128)S(1)}, s32[8]{0:T(128)}, u32[]{:S(2)}) copy-start(s32[8]{0:T(128)} %offsets_in.1) | copy-start | bytes 100
  2.8 0.7 %copy-start.2 = (s32[128]{0:T(128)S(1)}, s32[128]{0:T(128)}, u32[]{:S(2)}) copy-start(s32[128]{0:T(128)} %flips_in.1) | copy-start | bytes 1540

commit v3 on v2

--- a/solution.py
+++ b/solution.py
@@ -51,16 +51,15 @@
 def kernel(
     col_count, depth_count,
     dens, offsets_in, flips_in, out,
-    offsets, flips, weights, nat, ext, lrecv, rrecv, zsend, zrecv, crecv, lhs0, lhs1, res, kept,
+    offsets, flips, weights, ext, lrecv, rrecv, zsend, zrecv, crecv, lhs0, lhs1, res, kept,
     ysend, yrecv, isend, irecv, final, small_sem, in_sem, col_send, col_recv, z_send, z_recv, c_send, c_recv, y_send, y_recv, i_send, i_recv,
 ):
-    slices, columns, height = nat.shape
+    slices, columns, height = dens.shape
     absorb = 0.5 / (slices * depth_count)
     block = columns // depth_count
     pairs = depth_count // 2
     half = columns // 2
-    chunk = min(16, block)
-    group = min(4, chunk)
+    group = min(4, block)
     lump = min(4, block)
     col = lax.axis_index("col")
     depth = lax.axis_index("depth")
@@ -72,17 +71,21 @@
     def at(c, d):
         return {"col": c, "depth": d}
 
-    order = [0, slices - 1] + list(range(1, slices - 1))
-    loads = [pltpu.make_async_copy(dens.at[k], nat.at[k], in_sem.at[k]) for k in range(slices)]
-    for k in order:
-        loads[k].start()
+    def load(k, s):
+        return pltpu.make_async_copy(
+            dens.at[k, :, pl.ds(s * LANES, LANES)], ext.at[k + 1, pl.ds(LEFT, columns), s], in_sem.at[k, s]
+        )
+
+    for k in [0, slices - 1] + list(range(1, slices - 1)):
+        for s in range(SUB):
+            load(k, s).start()
 
     small = [
         pltpu.make_async_copy(offsets_in, offsets, small_sem.at[0]),
         pltpu.make_async_copy(flips_in, flips, small_sem.at[1]),
     ]
-    for load in small:
-        load.start()
+    for copy in small:
+        copy.start()
 
     barrier = pltpu.get_barrier_semaphore()
 
@@ -105,17 +108,6 @@
         pl.when(present & has_up)(lambda step=step: greet(col + step, depth - 1))
         pl.when(present & has_down)(lambda step=step: greet(col + step, depth + 1))
 
-    def move(k, x0):
-        ext[k + 1, pl.ds(LEFT + x0, 8)] = nat[k, pl.ds(x0, 8), :].reshape(8, SUB, LANES)
-
-    def relayout(k):
-        def body(i, carry):
-            for u in range(4):
-                move(k, pl.multiple_of(i * 32 + u * 8, 8))
-            return carry
-
-        lax.fori_loop(0, columns // 32, body, 0)
-
     def encode_slice(slot, k):
         def body(i, carry):
             low = ext[k + 1, pl.ds(LEFT + i * 8, 8)]
@@ -126,8 +118,8 @@
         lax.fori_loop(0, half // 8, body, 0)
 
     for k in (0, slices - 1):
-        loads[k].wait()
-        relayout(k)
+        for s in range(SUB):
+            load(k, s).wait()
     encode_slice(0, slices - 1)
     encode_slice(1, 0)
     pl.semaphore_wait(barrier, pairs - 1 + depth_sides + col_sides + col_sides * depth_sides)
@@ -153,25 +145,14 @@
         pl.when(z_out[slot] & has_right)(c_copies[slot].start)
 
     for k in range(1, slices - 1):
-        loads[k].wait()
-        for x0 in (0, columns - 16, columns - 8):
-            move(k, x0)
+        for s in range(SUB):
+            load(k, s).wait()
     inner = pl.ds(1, slices)
     to_right = remote(ext.at[inner, pl.ds(columns, LEFT)], lrecv, col_send.at[0], col_recv.at[0], col + 1, depth)
     to_left = remote(ext.at[inner, pl.ds(LEFT, 1)], rrecv, col_send.at[1], col_recv.at[1], col - 1, depth)
     pl.when(has_right)(to_right.start)
     pl.when(has_left)(to_left.start)
 
-    def relayout_inner(k, carry):
-        def body(i, inner_carry):
-            for u in range(4):
-                move(k, pl.multiple_of(8 + jnp.minimum(i * 32 + u * 8, columns - 32), 8))
-            return inner_carry
-
-        return lax.fori_loop(0, columns // 32, body, carry)
-
-    lax.fori_loop(1, slices - 1, relayout_inner, 0)
-
     source = lax.broadcasted_iota(jnp.int32, (LANES, LANES), 0)
     target = lax.broadcasted_iota(jnp.int32, (LANES, LANES), 1)
 
@@ -182,8 +163,8 @@
     weights[0:LANES, :] = taps(source - target).astype(jnp.bfloat16)
     shift = jnp.where(source < LANES // 2, LANES, -LANES)
     weights[LANES : 2 * LANES, :] = taps(source + shift - target).astype(jnp.bfloat16)
-    for load in small:
-        load.wait()
+    for copy in small:
+        copy.wait()
 
     shape = (group, SUB, LANES)
     lane = lax.broadcasted_iota(jnp.int32, shape, 2)
@@ -194,7 +175,7 @@
     edge_mask = jnp.where(low_lanes, not_last, not_first)
 
     def shade(k, x0, lhs):
-        for g in range(chunk // group):
+        for g in range(block // group):
             row = LEFT + x0 + g * group - offsets[k]
             rows = group * SUB
             window = [ext[k + 1, row + i] for i in range(-1, group + 1)]
@@ -213,13 +194,13 @@
             green = halved + halved * jnp.tanh(0.5 - 0.5 * center_sq)
             for ch, value in enumerate((halved + tilt, green, halved - tilt, opacity)):
                 edge = jnp.where(low_lanes, pltpu.roll(value, SUB - 1, 1), pltpu.roll(value, 1, 1)) * edge_mask
-                place = pl.ds((ch * chunk + g * group) * SUB, rows)
+                place = pl.ds((ch * block + g * group) * SUB, rows)
                 lhs[place, 0:LANES] = value.reshape(rows, LANES).astype(jnp.bfloat16)
                 lhs[place, LANES : 2 * LANES] = edge.reshape(rows, LANES).astype(jnp.bfloat16)
 
     def resample(k, x0, lhs):
         value = jnp.dot(lhs[...], weights[...], preferred_element_type=jnp.float32)
-        res[k, :, pl.ds(x0, chunk)] = value.reshape(4, chunk, SUB, LANES)
+        res[k, :, pl.ds(x0, block)] = value.reshape(4, block, SUB, LANES)
 
     def run(count, place):
         shade(*place(0), lhs0)
@@ -238,21 +219,24 @@
         lax.fori_loop(0, count // 2 - 1, body, 0)
         pair(count // 2 - 1, True)
 
-    chunks = columns // chunk
-    left_chunks = -(-LEFT // chunk)
-    mid_chunks = chunks - left_chunks - 1
-    rim_chunks = left_chunks + 1
+    left_blocks = -(-LEFT // block)
+    assert left_blocks % 2 == 1
+    mid_count = pairs - left_blocks // 2 - 1
+    rim_count = pairs - mid_count
+    mid_start = left_blocks // 2 + side
     mid_slices = slices - 2
-
-    def mid_place(t):
+    early = 2
+
+    def give_place(t, first, count):
         t = jnp.int32(t)
-        return 1 + t // mid_chunks, (left_chunks + lax.rem(t, mid_chunks)) * chunk
-
-    def rim_place(t):
+        slot = lax.rem(first + lax.rem(t, count), pairs)
+        return 1 + t // count, (2 * slot + 1 - side) * block
+
+    def keep_place(t, first):
         t = jnp.int32(t)
-        return 1 + t // rim_chunks, lax.rem(chunks - 1 + lax.rem(t, rim_chunks), chunks) * chunk
-
-    run(mid_slices * mid_chunks, mid_place)
+        return first + t // pairs, (2 * lax.rem(t, pairs) + side) * block
+
+    run(mid_slices * mid_count, lambda t: give_place(t, mid_start, mid_count))
 
     pl.when(has_right)(to_right.wait_send)
     pl.when(has_left)(to_left.wait_send)
@@ -275,7 +259,8 @@
     def _():
         ext[:, LEFT + columns : LEFT + columns + 1] = jnp.zeros((slices + 2, 1, SUB, LANES), jnp.float32)
 
-    run(mid_slices * rim_chunks, rim_place)
+    run(mid_slices * rim_count, lambda t: give_place(t, mid_start + mid_count, rim_count))
+    run(early * pairs, lambda t: keep_place(t, 1))
 
     def decode_slice(slot, plane):
         def body(i, carry):
@@ -303,11 +288,10 @@
 
     def finish_block(number):
         start = number * block
-        for i in range(block // chunk):
-            shade(0, start + i * chunk, lhs0)
-            resample(0, start + i * chunk, lhs0)
-            shade(slices - 1, start + i * chunk, lhs1)
-            resample(slices - 1, start + i * chunk, lhs1)
+        shade(0, start, lhs0)
+        resample(0, start, lhs0)
+        shade(slices - 1, start, lhs1)
+        resample(slices - 1, start, lhs1)
 
     def column_partial(x):
         flip = [flips[x + u] for u in range(lump)]
@@ -353,6 +337,7 @@
         return carry
 
     lax.fori_loop(0, pairs, give, 0)
+    run((mid_slices - early) * pairs, lambda t: keep_place(t, 1 + early))
 
     def keep(i, carry):
         slot = lax.rem(rank + 1 + i, pairs)
@@ -457,7 +442,6 @@
     slices, columns, height = density.shape
     block = columns // depth_count
     pairs = depth_count // 2
-    chunk = min(16, block)
     half = columns // 2
     f32, i32 = jnp.float32, jnp.int32
     dma = pltpu.SemaphoreType.DMA
@@ -466,21 +450,20 @@
         pltpu.SMEM((slices,), i32),
         pltpu.SMEM((columns,), i32),
         pltpu.VMEM((2 * LANES, LANES), jnp.bfloat16),
-        pltpu.VMEM((slices, columns, height), f32),
         pltpu.VMEM((slices + 2, LEFT + columns + 1, SUB, LANES), f32),
         pltpu.VMEM((slices, LEFT, SUB, LANES), f32),
         pltpu.VMEM((slices, 1, SUB, LANES), f32),
         pltpu.VMEM((2, half, SUB, LANES), i32),
         pltpu.VMEM((2, half, SUB, LANES), i32),
         pltpu.VMEM((2, SMAX, SUB, LANES), i32),
-        pltpu.VMEM((4 * chunk * SUB, 2 * LANES), jnp.bfloat16),
-        pltpu.VMEM((4 * chunk * SUB, 2 * LANES), jnp.bfloat16),
+        pltpu.VMEM((4 * block * SUB, 2 * LANES), jnp.bfloat16),
+        pltpu.VMEM((4 * block * SUB, 2 * LANES), jnp.bfloat16),
         pltpu.VMEM((slices, 4, columns, SUB, LANES), f32),
         pltpu.VMEM((4, block, SUB, LANES), f32),
         image, image, image, image,
         pltpu.VMEM((4, block, SUB, LANES), f32),
         dma((2,)),
-        dma((slices,)),
+        dma((slices, SUB)),
         dma((2,)), dma((2,)), dma((2,)), dma((2,)), dma((2,)), dma((2,)),
         dma((pairs,)), dma((pairs,)), dma((pairs,)), dma((pairs,)),
     ]
@@ -493,7 +476,7 @@
         out_specs=vmem,
         scratch_shapes=scratch,
         compiler_params=pltpu.CompilerParams(
-            collective_id=0, has_side_effects=True, vmem_limit_bytes=48 * 2**20
+            collective_id=0, has_side_effects=True, vmem_limit_bytes=63 * 2**20
         ),
     )(density, offsets, view_flip)
 

time: 42.4 us -> 44.3 us (1.045)
  the two profiles are of different devices: /device:TPU:0 before, /device:TPU:10 now
where the time goes in v3:
time: 44.3 us; the launch traced here: 44.1 us
  Pallas kernels  42.5 us (96%)
  local copies, waits for them, and re-layouts  1.67 us (4%)
    pallas_call x1, Pallas kernels, on_device(): pl.pallas_call(functools.partial(kernel, col_count, depth_count), out_sha...  42.5 us
    unnamed x1, local copies, waits for them, and re-layouts  1.67 us

profile of v3, /device:TPU:10, one launch (start us, length us, event | category | flops | bytes accessed | tf_op | source)
XLA Modules:
  0.0 44.1 jit_solution(9818050124548033966)
XLA Ops:
  0.0 42.5 %shard_map.37 = f32[4,16,1024]{2,1,0:T(8,128)} custom-call(f32[8,128,1024]{2,1,0:T(8,128)} %dens.1, s32[8]{0:T(128)} %offsets_in.1, s32[128]{0:T(128)} %flips_in.1), custom_call_target="tpu_custom_call" | custom-call | tf_op jit(solution)/shard_map/pallas_call | solution.py:472
  42.5 1.7 %copy.5 = f32[4,16,1024]{2,1,0:T(8,128)} copy(f32[4,16,1024]{2,1,0:T(8,128)} %shard_map.37) | data formatting | bytes 524288

commit v4 on v3

--- a/solution.py
+++ b/solution.py
@@ -51,7 +51,7 @@
 def kernel(
     col_count, depth_count,
     dens, offsets_in, flips_in, out,
-    offsets, flips, weights, ext, lrecv, rrecv, zsend, zrecv, crecv, lhs0, lhs1, res, kept,
+    offsets, flips, weights, nat, ext, lrecv, rrecv, zsend, zrecv, crecv, lhs0, lhs1, res, kept,
     ysend, yrecv, isend, irecv, final, small_sem, in_sem, col_send, col_recv, z_send, z_recv, c_send, c_recv, y_send, y_recv, i_send, i_recv,
 ):
     slices, columns, height = dens.shape
@@ -71,14 +71,9 @@
     def at(c, d):
         return {"col": c, "depth": d}
 
-    def load(k, s):
-        return pltpu.make_async_copy(
-            dens.at[k, :, pl.ds(s * LANES, LANES)], ext.at[k + 1, pl.ds(LEFT, columns), s], in_sem.at[k, s]
-        )
-
+    loads = [pltpu.make_async_copy(dens.at[k], nat.at[k], in_sem.at[k]) for k in range(slices)]
     for k in [0, slices - 1] + list(range(1, slices - 1)):
-        for s in range(SUB):
-            load(k, s).start()
+        loads[k].start()
 
     small = [
         pltpu.make_async_copy(offsets_in, offsets, small_sem.at[0]),
@@ -108,6 +103,17 @@
         pl.when(present & has_up)(lambda step=step: greet(col + step, depth - 1))
         pl.when(present & has_down)(lambda step=step: greet(col + step, depth + 1))
 
+    def move(k, x0):
+        ext[k + 1, pl.ds(LEFT + x0, 8)] = nat[k, pl.ds(x0, 8), :].reshape(8, SUB, LANES)
+
+    def relayout(k):
+        def body(i, carry):
+            for u in range(4):
+                move(k, pl.multiple_of(i * 32 + u * 8, 8))
+            return carry
+
+        lax.fori_loop(0, columns // 32, body, 0)
+
     def encode_slice(slot, k):
         def body(i, carry):
             low = ext[k + 1, pl.ds(LEFT + i * 8, 8)]
@@ -118,8 +124,8 @@
         lax.fori_loop(0, half // 8, body, 0)
 
     for k in (0, slices - 1):
-        for s in range(SUB):
-            load(k, s).wait()
+        loads[k].wait()
+        relayout(k)
     encode_slice(0, slices - 1)
     encode_slice(1, 0)
     pl.semaphore_wait(barrier, pairs - 1 + depth_sides + col_sides + col_sides * depth_sides)
@@ -145,13 +151,24 @@
         pl.when(z_out[slot] & has_right)(c_copies[slot].start)
 
     for k in range(1, slices - 1):
-        for s in range(SUB):
-            load(k, s).wait()
+        loads[k].wait()
+        for x0 in (0, columns - 16, columns - 8):
+            move(k, x0)
     inner = pl.ds(1, slices)
     to_right = remote(ext.at[inner, pl.ds(columns, LEFT)], lrecv, col_send.at[0], col_recv.at[0], col + 1, depth)
     to_left = remote(ext.at[inner, pl.ds(LEFT, 1)], rrecv, col_send.at[1], col_recv.at[1], col - 1, depth)
     pl.when(has_right)(to_right.start)
     pl.when(has_left)(to_left.start)
+
+    def relayout_inner(k, carry):
+        def body(i, inner_carry):
+            for u in range(4):
+                move(k, pl.multiple_of(8 + jnp.minimum(i * 32 + u * 8, columns - 32), 8))
+            return inner_carry
+
+        return lax.fori_loop(0, columns // 32, body, carry)
+
+    lax.fori_loop(1, slices - 1, relayout_inner, 0)
 
     source = lax.broadcasted_iota(jnp.int32, (LANES, LANES), 0)
     target = lax.broadcasted_iota(jnp.int32, (LANES, LANES), 1)
@@ -450,6 +467,7 @@
         pltpu.SMEM((slices,), i32),
         pltpu.SMEM((columns,), i32),
         pltpu.VMEM((2 * LANES, LANES), jnp.bfloat16),
+        pltpu.VMEM((slices, columns, height), f32),
         pltpu.VMEM((slices + 2, LEFT + columns + 1, SUB, LANES), f32),
         pltpu.VMEM((slices, LEFT, SUB, LANES), f32),
         pltpu.VMEM((slices, 1, SUB, LANES), f32),
@@ -463,7 +481,7 @@
         image, image, image, image,
         pltpu.VMEM((4, block, SUB, LANES), f32),
         dma((2,)),
-        dma((slices, SUB)),
+        dma((slices,)),
         dma((2,)), dma((2,)), dma((2,)), dma((2,)), dma((2,)), dma((2,)),
         dma((pairs,)), dma((pairs,)), dma((pairs,)), dma((pairs,)),
     ]

time: 44.3 us -> 43.6 us (0.984)
  Pallas kernels: 42.5 us -> 41.7 us
    pallas_call x1, Pallas kernels: 42.5 us -> 41.7 us  [on_device(): pl.pallas_call(functools.partial(kernel, col_count, depth_count), out_sha...]
where the time goes in v4:
time: 43.6 us; the launch traced here: 43.4 us
  Pallas kernels  41.7 us (96%)
  local copies, waits for them, and re-layouts  1.67 us (4%)
    pallas_call x1, Pallas kernels, on_device(): pl.pallas_call(functools.partial(kernel, col_count, depth_count), out_sha...  41.7 us
    unnamed x1, local copies, waits for them, and re-layouts  1.67 us

profile of v4, /device:TPU:10, one launch (start us, length us, event | category | flops | bytes accessed | tf_op | source)
XLA Modules:
  0.0 43.4 jit_solution(6543942756298179866)
XLA Ops:
  0.0 41.7 %shard_map.37 = f32[4,16,1024]{2,1,0:T(8,128)} custom-call(f32[8,128,1024]{2,1,0:T(8,128)} %dens.1, s32[8]{0:T(128)} %offsets_in.1, s32[128]{0:T(128)} %flips_in.1), custom_call_target="tpu_custom_call" | custom-call | tf_op jit(solution)/shard_map/pallas_call | solution.py:490
  41.7 1.7 %copy.5 = f32[4,16,1024]{2,1,0:T(8,128)} copy(f32[4,16,1024]{2,1,0:T(8,128)} %shard_map.37) | data formatting | bytes 524288

commit v5 on v4

--- a/solution.py
+++ b/solution.py
@@ -59,7 +59,7 @@
     block = columns // depth_count
     pairs = depth_count // 2
     half = columns // 2
-    group = min(4, block)
+    group = min(2, block)
     lump = min(4, block)
     col = lax.axis_index("col")
     depth = lax.axis_index("depth")
@@ -184,12 +184,14 @@
         copy.wait()
 
     shape = (group, SUB, LANES)
-    lane = lax.broadcasted_iota(jnp.int32, shape, 2)
-    sub = lax.broadcasted_iota(jnp.int32, shape, 1)
-    not_first = jnp.where(sub == 0, 0.0, 1.0)
-    not_last = jnp.where(sub == SUB - 1, 0.0, 1.0)
-    low_lanes = lane < LANES // 2
-    edge_mask = jnp.where(low_lanes, not_last, not_first)
+    lane = lax.broadcasted_iota(jnp.int32, (SUB, LANES), 1)
+    sub = lax.broadcasted_iota(jnp.int32, (SUB, LANES), 0)
+    not_first = jnp.where(sub == 0, 0.0, 1.0)[None]
+    not_last = jnp.where(sub == SUB - 1, 0.0, 1.0)[None]
+    edge_mask = jnp.where(lane < LANES // 2, not_last[0], not_first[0])[None]
+
+    def pick(mask, first, second):
+        return jnp.where(jnp.broadcast_to(mask[None], first.shape), first, second)
 
     def shade(k, x0, lhs):
         for g in range(block // group):
@@ -199,8 +201,8 @@
             center = jnp.stack(window[1:-1])
             dx = jnp.stack(window[2:]) - jnp.stack(window[:-2])
             dz = jnp.stack([ext[k + 2, row + i] - ext[k, row + i] for i in range(group)])
-            before = jnp.where(lane == LANES - 1, pltpu.roll(center, 1, 1) * not_first, center)
-            after = jnp.where(lane == 0, pltpu.roll(center, SUB - 1, 1) * not_last, center)
+            before = pick(lane == LANES - 1, pltpu.roll(center, 1, 1) * not_first, center)
+            after = pick(lane == 0, pltpu.roll(center, SUB - 1, 1) * not_last, center)
             dy = pltpu.roll(after, LANES - 1, 2) - pltpu.roll(before, 1, 2)
             square = dx * dx + dy * dy + dz * dz
             lambert = (0.48 * dx + 0.6 * dy + 0.64 * dz) * lax.rsqrt(jnp.maximum(square, 4.0))
@@ -210,7 +212,7 @@
             tilt = halved * jnp.tanh(center)
             green = halved + halved * jnp.tanh(0.5 - 0.5 * center_sq)
             for ch, value in enumerate((halved + tilt, green, halved - tilt, opacity)):
-                edge = jnp.where(low_lanes, pltpu.roll(value, SUB - 1, 1), pltpu.roll(value, 1, 1)) * edge_mask
+                edge = pick(lane < LANES // 2, pltpu.roll(value, SUB - 1, 1), pltpu.roll(value, 1, 1)) * edge_mask
                 place = pl.ds((ch * block + g * group) * SUB, rows)
                 lhs[place, 0:LANES] = value.reshape(rows, LANES).astype(jnp.bfloat16)
                 lhs[place, LANES : 2 * LANES] = edge.reshape(rows, LANES).astype(jnp.bfloat16)
@@ -343,13 +345,9 @@
         number = 2 * slot + 1 - side
         finish_block(number)
 
-        def body(step, inner_carry):
-            x = step * lump
+        for x in range(0, block, lump):
             colour, transmit = column_partial(number * block + x)
             store_codes(ysend, slot, x, colour, 1.0 - transmit)
-            return inner_carry
-
-        lax.fori_loop(0, block // lump, body, 0)
         y_copy(slot).start()
         return carry
 
@@ -361,19 +359,14 @@
         number = 2 * slot + side
         finish_block(number)
 
-        def body(step, inner_carry):
-            x = step * lump
+        for x in range(0, block, lump):
             colour, transmit = column_partial(number * block + x)
             for ch in range(3):
                 kept[ch, pl.ds(x, lump)] = colour[ch]
             kept[3, pl.ds(x, lump)] = transmit
-            return inner_carry
-
-        lax.fori_loop(0, block // lump, body, 0)
         y_copy(slot).wait_recv()
 
-        def join(step, inner_carry):
-            x = step * lump
+        for x in range(0, block, lump):
             span = pl.ds(x, lump)
             theirs, their_opacity = load_codes(yrecv[slot, 0, span], yrecv[slot, 1, span])
             their_transmit = 1.0 - their_opacity
@@ -389,17 +382,8 @@
                 colour.append(front + front_transmit * behind)
             opacity = 1.0 - my_transmit * their_transmit
 
-            @pl.when(i < pairs - 1)
-            def _():
-                store_codes(isend, slot, x, colour, opacity)
-
-            @pl.when(i == pairs - 1)
-            def _():
-                store_codes(irecv, rank, x, colour, opacity)
-
-            return inner_carry
-
-        lax.fori_loop(0, block // lump, join, 0)
+            store_codes(isend, slot, x, colour, opacity)
+            store_codes(irecv, rank, x, colour, opacity)
         pl.when(i < pairs - 1)(lambda: i_copy(slot).start())
         return carry
 
@@ -414,8 +398,7 @@
 
     lax.fori_loop(1, pairs, arrive, 0)
 
-    def compose(step, carry):
-        x = step * lump
+    for x in range(0, block, lump):
         flip = [flips[depth * block + x + u] for u in range(lump)]
         colour = [None] * 3
         transmit = None
@@ -429,9 +412,6 @@
         for ch in range(3):
             final[ch, pl.ds(x, lump)] = colour[ch]
         final[3, pl.ds(x, lump)] = 1.0 - transmit
-        return carry
-
-    lax.fori_loop(0, block // lump, compose, 0)
     part = min(8, block)
     for ch in range(4):
         for x0 in range(0, block, part):

time: 43.6 us -> 43 us (0.986)
  Pallas kernels: 41.7 us -> 41.2 us
    pallas_call x1, Pallas kernels: 41.7 us -> 41.2 us  [on_device(): pl.pallas_call(functools.partial(kernel, col_count, depth_count), out_sha...]
where the time goes in v5:
time: 43 us; the launch traced here: 42.9 us
  Pallas kernels  41.2 us (96%)
  local copies, waits for them, and re-layouts  1.67 us (4%)
    pallas_call x1, Pallas kernels, on_device(): pl.pallas_call(functools.partial(kernel, col_count, depth_count), out_sha...  41.2 us
    unnamed x1, local copies, waits for them, and re-layouts  1.67 us

profile of v5, /device:TPU:10, one launch (start us, length us, event | category | flops | bytes accessed | tf_op | source)
XLA Modules:
  0.0 42.9 jit_solution(14012599893137869672)
XLA Ops:
  0.0 41.2 %shard_map.37 = f32[4,16,1024]{2,1,0:T(8,128)} custom-call(f32[8,128,1024]{2,1,0:T(8,128)} %dens.1, s32[8]{0:T(128)} %offsets_in.1, s32[128]{0:T(128)} %flips_in.1), custom_call_target="tpu_custom_call" | custom-call | tf_op jit(solution)/shard_map/pallas_call | solution.py:470
  41.2 1.7 %copy.5 = f32[4,16,1024]{2,1,0:T(8,128)} copy(f32[4,16,1024]{2,1,0:T(8,128)} %shard_map.37) | data formatting | bytes 524288

commit v6 on v5

--- a/solution.py
+++ b/solution.py
@@ -114,10 +114,21 @@
 
         lax.fori_loop(0, columns // 32, body, 0)
 
+    groups = half // 8
+    late = 2 if block == 2 * SMAX and groups == 8 else 0
+    first = (groups - late) * 8
+
+    def group_at(i, parity):
+        if not late:
+            return i
+        skipped = lax.rem(2 - 2 * parity + 4 * (i - 6) + 8, 8)
+        return jnp.where(i < 6, lax.rem(2 - 2 * parity + i + 1 + i // 3, 8), skipped)
+
     def encode_slice(slot, k):
         def body(i, carry):
-            low = ext[k + 1, pl.ds(LEFT + i * 8, 8)]
-            high = ext[k + 1, pl.ds(LEFT + half + i * 8, 8)]
+            g = group_at(i, side)
+            low = ext[k + 1, pl.ds(LEFT + g * 8, 8)]
+            high = ext[k + 1, pl.ds(LEFT + half + g * 8, 8)]
             zsend[slot, pl.ds(i * 8, 8)] = pack(density_code(low), density_code(high))
             return carry
 
@@ -135,10 +146,14 @@
             src_ref=src, dst_ref=dst, send_sem=send, recv_sem=recv, device_id=at(c, d), device_id_type=MESH
         )
 
-    tail = pl.ds(half - SMAX, SMAX)
+    tail = pl.ds((3 + 2 * side) * 8 if late else half - SMAX, SMAX)
+    parts = [(0, pl.ds(0, first))] + ([(1, pl.ds(first, late * 8))] if late else [])
     z_copies = [
-        remote(zsend.at[0], zrecv.at[0], z_send.at[0], z_recv.at[0], col, depth + 1),
-        remote(zsend.at[1], zrecv.at[1], z_send.at[1], z_recv.at[1], col, depth - 1),
+        [
+            remote(zsend.at[slot, span], zrecv.at[slot, span], z_send.at[slot, n], z_recv.at[slot, n], col, to)
+            for n, span in parts
+        ]
+        for slot, to in ((0, depth + 1), (1, depth - 1))
     ]
     c_copies = [
         remote(zsend.at[0, tail], crecv.at[0], c_send.at[0], c_recv.at[0], col + 1, depth + 1),
@@ -147,8 +162,10 @@
     z_out = (has_down, has_up)
     z_in = (has_up, has_down)
     for slot in range(2):
-        pl.when(z_out[slot])(z_copies[slot].start)
+        pl.when(z_out[slot])(z_copies[slot][0].start)
         pl.when(z_out[slot] & has_right)(c_copies[slot].start)
+    for slot in range(2 if late else 0):
+        pl.when(z_out[slot])(z_copies[slot][1].start)
 
     for k in range(1, slices - 1):
         loads[k].wait()
@@ -281,20 +298,21 @@
     run(mid_slices * rim_count, lambda t: give_place(t, mid_start + mid_count, rim_count))
     run(early * pairs, lambda t: keep_place(t, 1))
 
-    def decode_slice(slot, plane):
+    def decode_slice(slot, plane, start, stop):
         def body(i, carry):
+            g = group_at(i, 1 - side)
             word = zrecv[slot, pl.ds(i * 8, 8)]
-            ext[plane, pl.ds(LEFT + i * 8, 8)] = density_value(low_half(word))
-            ext[plane, pl.ds(LEFT + half + i * 8, 8)] = density_value(high_half(word))
+            ext[plane, pl.ds(LEFT + g * 8, 8)] = density_value(low_half(word))
+            ext[plane, pl.ds(LEFT + half + g * 8, 8)] = density_value(high_half(word))
             return carry
 
-        lax.fori_loop(0, half // 8, body, 0)
+        lax.fori_loop(start, stop, body, 0)
 
     for slot, plane in ((0, 0), (1, slices + 1)):
         @pl.when(z_in[slot])
         def _(slot=slot, plane=plane):
-            z_copies[slot].wait_recv()
-            decode_slice(slot, plane)
+            z_copies[slot][0].wait_recv()
+            decode_slice(slot, plane, 0, groups - late)
 
         @pl.when(z_in[slot] & has_left)
         def _(slot=slot, plane=plane):
@@ -352,6 +370,12 @@
         return carry
 
     lax.fori_loop(0, pairs, give, 0)
+    for slot, plane in ((0, 0), (1, slices + 1)) if late else ():
+        @pl.when(z_in[slot])
+        def _(slot=slot, plane=plane):
+            z_copies[slot][1].wait_recv()
+            decode_slice(slot, plane, groups - late, groups)
+
     run((mid_slices - early) * pairs, lambda t: keep_place(t, 1 + early))
 
     def keep(i, carry):
@@ -418,7 +442,8 @@
             out[ch, x0 : x0 + part, :] = final[ch, x0 : x0 + part].reshape(part, height)
 
     for slot in range(2):
-        pl.when(z_out[slot])(z_copies[slot].wait_send)
+        for copy in z_copies[slot]:
+            pl.when(z_out[slot])(copy.wait_send)
         pl.when(z_out[slot] & has_right)(c_copies[slot].wait_send)
 
     def left_y(i, carry):
@@ -462,7 +487,7 @@
         pltpu.VMEM((4, block, SUB, LANES), f32),
         dma((2,)),
         dma((slices,)),
-        dma((2,)), dma((2,)), dma((2,)), dma((2,)), dma((2,)), dma((2,)),
+        dma((2,)), dma((2,)), dma((2, 2)), dma((2, 2)), dma((2,)), dma((2,)),
         dma((pairs,)), dma((pairs,)), dma((pairs,)), dma((pairs,)),
     ]
     vmem = pl.BlockSpec(memory_space=pltpu.VMEM)
@@ -474,7 +499,7 @@
         out_specs=vmem,
         scratch_shapes=scratch,
         compiler_params=pltpu.CompilerParams(
-            collective_id=0, has_side_effects=True, vmem_limit_bytes=63 * 2**20
+            collective_id=0, has_side_effects=True, vmem_limit_bytes=48 * 2**20
         ),
     )(density, offsets, view_flip)
 

time: 43 us -> 44.3 us (1.030)
  local copies, waits for them, and re-layouts: 1.67 us -> 4.2 us
  Pallas kernels: 41.2 us -> 39.6 us
    unnamed x1 -> x7, local copies, waits for them, and re-layouts: 1.67 us -> 4.2 us
    pallas_call x1, Pallas kernels: 41.2 us -> 39.6 us  [on_device(): pl.pallas_call(functools.partial(kernel, col_count, depth_count), out_sha...]
where the time goes in v6:
time: 44.3 us; the launch traced here: 43.8 us
  Pallas kernels  39.6 us (89%)
  local copies, waits for them, and re-layouts  4.2 us (9%)
    pallas_call x1, Pallas kernels, on_device(): pl.pallas_call(functools.partial(kernel, col_count, depth_count), out_sha...  39.6 us
    unnamed x7, local copies, waits for them, and re-layouts  4.2 us

profile of v6, /device:TPU:10, one launch (start us, length us, event | category | flops | bytes accessed | tf_op | source)
XLA Modules:
  0.0 43.8 jit_solution(3361911873044272504)
XLA Ops:
  0.0 0.0 copy-start
  0.0 2.2 %copy-done = f32[8,128,1024]{2,1,0:T(8,128)S(1)} copy-done((f32[8,128,1024]{2,1,0:T(8,128)S(1)}, f32[8,128,1024]{2,1,0:T(8,128)}, u32[]{:S(2)}) %copy-start) | copy-done | bytes 4194328
  2.2 0.0 copy-start.1
  2.2 0.7 %copy-done.1 = s32[8]{0:T(128)S(1)} copy-done((s32[8]{0:T(128)S(1)}, s32[8]{0:T(128)}, u32[]{:S(2)}) %copy-start.1) | copy-done | bytes 56
  2.8 0.0 copy-start.2
  2.8 0.7 %copy-done.2 = s32[128]{0:T(128)S(1)} copy-done((s32[128]{0:T(128)S(1)}, s32[128]{0:T(128)}, u32[]{:S(2)}) %copy-start.2) | copy-done | bytes 536
  3.5 39.6 %shard_map.37 = f32[4,16,1024]{2,1,0:T(8,128)S(1)} custom-call(f32[8,128,1024]{2,1,0:T(8,128)S(1)} %copy-done, s32[8]{0:T(128)S(1)} %copy-done.1, s32[128]{0:T(128)S(1)} %copy-done.2), custom_call_target="tpu_custom_call" | custom-call | tf_op jit(solution)/shard_map/pallas_call | solution.py:495
  43.1 0.7 %copy.5 = f32[4,16,1024]{2,1,0:T(8,128)} copy(f32[4,16,1024]{2,1,0:T(8,128)S(1)} %shard_map.37) | data formatting | bytes 524288
Async XLA Ops:
  0.0 2.2 %copy-start = (f32[8,128,1024]{2,1,0:T(8,128)S(1)}, f32[8,128,1024]{2,1,0:T(8,128)}, u32[]{:S(2)}) copy-start(f32[8,128,1024]{2,1,0:T(8,128)} %dens.1) | copy-start | bytes 12582916
  2.2 0.7 %copy-start.1 = (s32[8]{0:T(128)S(1)}, s32[8]{0:T(128)}, u32[]{:S(2)}) copy-start(s32[8]{0:T(128)} %offsets_in.1) | copy-start | bytes 100
  2.8 0.7 %copy-start.2 = (s32[128]{0:T(128)S(1)}, s32[128]{0:T(128)}, u32[]{:S(2)}) copy-start(s32[128]{0:T(128)} %flips_in.1) | copy-start | bytes 1540
